TPU v7x, 512 devices: a whole 4x8x8 slice. The times are simulated.
512 devices in a mesh: seq: 32 (over y_hi, z, core), tensor: 16 (over y_lo, x).
Axes of the slice: x: 4, y: 8 (y_hi: 2, y_lo: 4; y = y_hi * 4 + y_lo), z: 8, core: 2. Of those that a mesh axis runs over, the one named last changes fastest.
Arguments:
- tokens: bfloat16 [8192, 2304], P('seq'), may hold values from -6 to 6
- target: bfloat16 [8192, 2304], P('seq'), may hold values from -6 to 6
- segment_ids: int32 [8192], P('seq'), may hold values from 0 to 31, never falling along the last dimension, each value on 1 to 1024 neighbouring positions
- norm_gain: float32 [2304], replicated, may hold values from 0.1 to 1.9
- w_gate: bfloat16 [2304, 4608], P('seq', 'tensor'), may hold values from -0.125 to 0.125
- w_up: bfloat16 [2304, 4608], P('seq', 'tensor'), may hold values from -0.125 to 0.125
- w_down: bfloat16 [4608, 2304], P('tensor', 'seq'), may hold values from -0.09375 to 0.09375
- dir_gate: bfloat16 [2304, 4608], P('seq', 'tensor'), may hold values from -4 to 4
- dir_up: bfloat16 [2304, 4608], P('seq', 'tensor'), may hold values from -4 to 4
- dir_down: bfloat16 [4608, 2304], P('tensor', 'seq'), may hold values from -4 to 4
- ema_gate: float32 [2304, 4608], P('seq', 'tensor'), may hold values from 0.05 to 2
- ema_up: float32 [2304, 4608], P('seq', 'tensor'), may hold values from 0.05 to 2
- ema_down: float32 [4608, 2304], P('tensor', 'seq'), may hold values from 0.05 to 2
Outputs:
- new_gate: float32 [2304, 4608], P('seq', 'tensor')
- new_up: float32 [2304, 4608], P('seq', 'tensor')
- new_down: float32 [4608, 2304], P('tensor', 'seq')
Inputs may be any that keep to these rules, and one draw needn't show every extreme that they name: `segment_ids`: ids never fall along the pack; each of the 32 documents has 1 to 1024 tokens, and one has exactly 1024.
All inputs are finite; a program needn't handle non-finite values.
Results may differ from a plain program's by a relative error of at most 0.025.
Values may be sent and summed in bfloat16 or wider, within the bound.
No kernel may reach another device: no remote copies, remote signals or barrier semaphores. Data moves between devices by JAX's collectives and lax.ppermute only.
A program may use at most 64 MiB of HBM per device.

v0:
```python
import jax
import jax.numpy as jnp
from jax import lax
from jax.sharding import PartitionSpec as P

gelu_rate = 0.7978845608028654
gelu_cubic = 0.044715
beta_decay = 0.9
norm_eps = 1e-06

NZ = 8
ROWS = 72
UNITS = 288
TALLY = 64
BF = jnp.bfloat16
F32 = jnp.float32


def gelu_parts(pre):
    inner = gelu_rate * (pre + gelu_cubic * pre * pre * pre)
    slope = gelu_rate * (1.0 + 3.0 * gelu_cubic * pre * pre)
    bend = 6.0 * gelu_rate * gelu_cubic * pre
    tanh_val = jnp.tanh(inner)
    sech_sq = 1.0 - tanh_val * tanh_val
    value = 0.5 * pre * (1.0 + tanh_val)
    first = 0.5 * (1.0 + tanh_val) + 0.5 * pre * sech_sq * slope
    second = sech_sq * (slope + 0.5 * pre * (bend - 2.0 * tanh_val * slope * slope))
    return (value, first, second)


def product(left, right):
    return jnp.dot(left, right, preferred_element_type=F32)


def against(left, right):
    return lax.dot_general(left, right, (((1,), (1,)), ((), ())), preferred_element_type=F32)


def over_tokens(left, right):
    return lax.dot_general(left, right, (((0,), (0,)), ((), ())), preferred_element_type=F32)


def blend(ema, probe, hvp):
    return beta_decay * ema + (1.0 - beta_decay) * (probe.astype(F32) * hvp)


def ring_step(array):
    perm = [
        (s, (s // 16) * 16 + ((s // 2 % 8 + (1 - 2 * (s % 2))) % 8) * 2 + s % 2) for s in range(32)
    ]
    return lax.ppermute(array, "seq", perm)


def seq_swap(array, bit):
    return lax.ppermute(array, "seq", [(s, s ^ bit) for s in range(32)])


def y_swap(array, bit):
    return lax.ppermute(array, "tensor", [(t, t ^ (bit * 4)) for t in range(16)])


Z_GROUPS = [[y * 16 + z * 2 + c for z in range(8)] for y in range(2) for c in range(2)]
X_GROUPS = [[y * 4 + x for x in range(4)] for y in range(4)]
Y_GROUPS = [[y * 4 + x for y in range(4)] for x in range(4)]


def group_gather(array, axis, groups):
    return lax.all_gather(array, axis, axis_index_groups=groups)


def group_scatter(array, axis, groups):
    return lax.psum_scatter(array, axis, scatter_dimension=0, axis_index_groups=groups)


def group_exchange(array, axis, groups):
    return lax.all_to_all(array, axis, 0, 0, axis_index_groups=groups)


def after(array, *earlier):
    for other in earlier:
        array = array + 0 * other[(slice(0, 1),) * other.ndim].reshape((1,) * array.ndim)
    return array


def ring_chunks(chunk):
    held = [chunk]
    for k in range(1, NZ):
        held.append(ring_step(held[-1]))
    return held


def in_order(held, z, sign):
    own = jnp.zeros((NZ,) + held[0].shape, held[0].dtype)
    for k, chunk in enumerate(held):
        own = lax.dynamic_update_slice(own, chunk[None], ((z - sign * k) % NZ, 0, 0))
    return own


def exchange_sum(parts, axis, groups):
    return jnp.sum(group_exchange(parts, axis, groups).astype(F32), axis=0)


def x_shift(array, by):
    perm = [(t, (t // 4) * 4 + (t % 4 + by) % 4) for t in range(16)]
    return lax.ppermute(array, "tensor", perm)


def scatter_tensor(parts, x, y):
    n = parts[0].shape[1]
    h = n // 2
    parts = [part.reshape(4, 64, n) for part in parts]

    def block(part, at):
        return lax.dynamic_index_in_dim(part, (x + at) % 4, 0, keepdims=False)

    def add(left, right):
        return (left.astype(F32) + right.astype(F32)).astype(BF)

    def onward(part, up, down):
        ahead, behind = block(part, 1), block(part, 3)
        return (
            jnp.concatenate([add(ahead[:, :h], up), ahead[:, h:]], axis=1),
            jnp.concatenate([behind[:, :h], add(behind[:, h:], down)], axis=1),
        )

    far = [block(part, 2) for part in parts]
    ups = [x_shift(f[:, :h], 1) for f in far]
    downs = [x_shift(f[:, h:], -1) for f in far]
    pairs = [onward(*each) for each in zip(parts, ups, downs)]
    ups = [x_shift(up, 1) for up, _ in pairs]
    downs = [x_shift(down, -1) for _, down in pairs]
    low, high = y % 2, y // 2
    sums = [
        (block(part, 0).astype(F32) + up.astype(F32) + down.astype(F32)).reshape(2, 2, 16, n)
        for part, up, down in zip(parts, ups, downs)
    ]
    sent = [lax.dynamic_index_in_dim(s, 1 - low, 1, keepdims=False).astype(BF) for s in sums]
    got = [y_swap(s, 1) for s in sent]
    sums = [
        lax.dynamic_index_in_dim(s, low, 1, keepdims=False) + g.astype(F32)
        for s, g in zip(sums, got)
    ]
    sent = [lax.dynamic_index_in_dim(s, 1 - high, 0, keepdims=False).astype(BF) for s in sums]
    got = [y_swap(s, 2) for s in sent]
    return [
        lax.dynamic_index_in_dim(s, high, 0, keepdims=False) + g.astype(F32)
        for s, g in zip(sums, got)
    ]


def gather_tensor(owns, x, y):
    n = owns[0].shape[1]
    h = n // 2
    low, high = y % 2, y // 2
    others = [y_swap(own, 2) for own in owns]
    pairs = [
        jnp.where(high == 0, jnp.stack([own, other]), jnp.stack([other, own]))
        for own, other in zip(owns, others)
    ]
    others = [y_swap(pair, 1) for pair in pairs]
    rows = [
        jnp.where(
            low == 0, jnp.stack([pair, other], axis=1), jnp.stack([other, pair], axis=1)
        ).reshape(64, n)
        for pair, other in zip(pairs, others)
    ]

    def put(buf, piece, at, col=0):
        return lax.dynamic_update_slice(buf, piece[None], ((x + at) % 4, 0, col))

    ups = [x_shift(r, 1) for r in rows]
    downs = [x_shift(r, -1) for r in rows]
    far_ups = [x_shift(up[:, :h], 1) for up in ups]
    far_downs = [x_shift(down[:, h:], -1) for down in downs]
    result = []
    for own, up, down, far_up, far_down in zip(rows, ups, downs, far_ups, far_downs):
        buf = put(jnp.zeros((4, 64, n), own.dtype), own, 0)
        buf = put(put(buf, up, 3), down, 1)
        buf = put(put(buf, far_up, 2), far_down, 2, h)
        result.append(buf.reshape(256, n))
    return result


def relative(rows, y, c):
    m = rows.shape[0]
    parts = rows.reshape(m, 2, NZ, 2, ROWS).transpose(1, 3, 0, 2, 4).reshape(2, 2, m, NZ * ROWS)
    parts = jnp.where(y == 0, parts, parts[::-1])
    parts = jnp.where(c == 0, parts, parts[:, ::-1])
    return parts.transpose(2, 0, 1, 3).reshape(m, 4 * NZ * ROWS)


def per_device(
    tokens,
    target,
    segment_ids,
    norm_gain,
    w_gate,
    w_up,
    w_down,
    dir_gate,
    dir_up,
    dir_down,
    ema_gate,
    ema_up,
    ema_down,
):
    s = lax.axis_index("seq")
    t = lax.axis_index("tensor")
    yh, z, c = s // 16, (s // 2) % 8, s % 2
    yl, x = t // 4, t % 4

    sign = 1 - 2 * c
    labels = jnp.arange(32, dtype=jnp.int32)
    onehot = (segment_ids[:, None] == labels[None, :]).astype(F32)

    own_in = jnp.concatenate([w_gate, w_up, dir_gate, dir_up], axis=1)
    tally = jnp.pad(jnp.sum(onehot, axis=0).astype(BF)[None], ((0, ROWS - 1), (0, TALLY - 32)))
    own_out = jnp.concatenate([w_down.T, dir_down.T, tally], axis=1)
    across_in = seq_swap(own_in, 16)
    near_held = ring_chunks(own_in)
    near = in_order(near_held, z, sign)
    own_out = after(own_out, near_held[1])
    outs = group_gather(jnp.stack([own_out, seq_swap(own_out, 16)]), "seq", Z_GROUPS)
    near_other = seq_swap(near, 1)
    away = in_order(ring_chunks(across_in), z, sign)
    outs_other = seq_swap(outs, 1)
    away_other = seq_swap(away, 1)

    tokens = after(tokens, near_held[-1])
    target = after(target, near_held[-1])
    wide = tokens.astype(F32)
    scale = lax.rsqrt(jnp.mean(wide * wide, axis=1, keepdims=True) + norm_eps)
    normed = (wide * scale * norm_gain).astype(BF)
    normed = relative(normed, yh, c)

    half = 2 * NZ * ROWS
    near_all = jnp.stack([near, near_other]).reshape(half, 4 * UNITS)
    away_all = jnp.stack([away, away_other]).reshape(half, 4 * UNITS)
    pre = product(normed[:, :half], near_all) + product(normed[:, half:], away_all)
    gate, upper, gate_dot, upper_dot = (pre[:, i * UNITS : (i + 1) * UNITS] for i in range(4))
    value, first, second = gelu_parts(gate)
    hidden = (value * upper).astype(BF)
    hidden_dot = (first * gate_dot * upper + value * upper_dot).astype(BF)

    outs_all = jnp.stack([outs, outs_other]).transpose(2, 0, 1, 3, 4)
    counts = jnp.sum(outs_all[:, :, :, 0, 2 * UNITS : 2 * UNITS + 32].astype(F32), axis=(0, 1, 2))
    down_all = outs_all[..., : 2 * UNITS].reshape(4 * NZ * ROWS, 2 * UNITS)
    mixed_part = against(hidden, down_all[:, :UNITS]).astype(BF)
    mixed_dot_part = against(jnp.concatenate([hidden_dot, hidden], axis=1), down_all).astype(BF)
    mixed, mixed_dot = scatter_tensor([mixed_part, mixed_dot_part], x, yl)

    at = x * 64 + yl * 16
    my_tokens = relative(lax.dynamic_slice_in_dim(tokens, at, 16, 0), yh, c).astype(F32)
    my_target = relative(lax.dynamic_slice_in_dim(target, at, 16, 0), yh, c).astype(F32)
    my_hot = lax.dynamic_slice_in_dim(onehot, at, 16, 0)
    lengths = jnp.sum(my_hot * counts[None], axis=1, keepdims=True)
    my_grad = ((my_tokens + mixed - my_target) / lengths).astype(BF)
    my_grad_dot = (mixed_dot / lengths).astype(BF)
    grad_out, grad_out_dot = gather_tensor([my_grad, my_grad_dot], x, yl)

    back = product(grad_out, down_all)
    back_dot = product(grad_out_dot, down_all[:, :UNITS])
    grad_hidden = back[:, :UNITS]
    grad_hidden_dot = back_dot + back[:, UNITS:]
    grad_gate_dot = (
        (grad_hidden_dot * upper + grad_hidden * upper_dot) * first
        + grad_hidden * upper * second * gate_dot
    ).astype(BF)
    grad_upper_dot = (grad_hidden_dot * value + grad_hidden * first * gate_dot).astype(BF)
    grads = jnp.concatenate([grad_gate_dot, grad_upper_dot], axis=1)

    def terms(lo):
        rows = slice(lo, lo + half)
        part_in = over_tokens(normed[:, rows], grads).astype(BF)
        part_out = (
            over_tokens(grad_out[:, rows], hidden_dot) + over_tokens(grad_out_dot[:, rows], hidden)
        ).astype(BF)
        part = jnp.concatenate([part_in, part_out], axis=1).reshape(2, NZ, ROWS, 3 * UNITS)
        return (part[0].astype(F32) + seq_swap(part[1], 1).astype(F32)).astype(BF)

    near_terms = terms(0)
    away_terms = terms(half)
    near_tail = group_scatter(near_terms[..., UNITS:], "seq", Z_GROUPS).astype(F32)
    sums = exchange_sum(
        jnp.concatenate([away_terms, near_terms[..., :UNITS]], axis=2), "seq", Z_GROUPS
    )
    away_sum = seq_swap(sums[:, : 3 * UNITS].astype(BF), 16).astype(F32)
    hvp = jnp.concatenate([sums[:, 3 * UNITS :], near_tail], axis=1) + away_sum
    return (
        blend(ema_gate, dir_gate, hvp[:, :UNITS]),
        blend(ema_up, dir_up, hvp[:, UNITS : 2 * UNITS]),
        blend(ema_down, dir_down, hvp[:, 2 * UNITS :].T),
    )


def solution(mesh):
    in_specs = (
        P("seq", None),
        P("seq", None),
        P("seq"),
        P(),
        P("seq", "tensor"),
        P("seq", "tensor"),
        P("tensor", "seq"),
        P("seq", "tensor"),
        P("seq", "tensor"),
        P("tensor", "seq"),
        P("seq", "tensor"),
        P("seq", "tensor"),
        P("tensor", "seq"),
    )
    out_specs = (P("seq", "tensor"), P("seq", "tensor"), P("tensor", "seq"))
    return jax.shard_map(
        per_device, mesh=mesh, in_specs=in_specs, out_specs=out_specs, check_vma=False
    )
```

profile of v0, /device:TPU:56, one launch (start us, length us, event | category | flops | bytes accessed | tf_op | source)
XLA Modules:
  0.0 309.5 jit_solution(5239304606017598773)
XLA Ops:
  8.4 4.3 %collective-permute-start = (bf16[72,1152]{1,0:T(8,128)(2,1)S(1)}, bf16[72,1152]{1,0:T(8,128)(2,1)}, u32[]{:S(2)}, u32[]{:S(2)}) collective-permute-start(bf16[72,1152]{1,0:T(8,128)(2,1)S(1)} %concatenate.79), channel_id=1, source_target_pairs={{0,32},{16,240},{32,64},{48,16},{64,96},{80,48},{96,128},{112,80},... | collective-permute-start | bytes 497672 | tf_op jit(solution)/shard_map/ppermute | solution.py:51
  12.7 4.7 %collective-permute-start.8 = (bf16[72,1152]{1,0:T(8,128)(2,1)S(1)}, bf16[72,1152]{1,0:T(8,128)(2,1)S(1)}, u32[]{:S(2)}, u32[]{:S(2)}) collective-permute-start(bf16[72,1152]{1,0:T(8,128)(2,1)S(1)} %concatenate.79), channel_id=1, source_target_pairs={{0,256},{16,272},{32,288},{48,304},{64,320},{80,336},{96,352},{112... | collective-permute-start | bytes 497672 | tf_op jit(solution)/shard_map/ppermute | solution.py:55
  24.8 4.8 %collective-permute-start.17 = (bf16[72,640]{1,0:T(8,128)(2,1)S(1)}, bf16[72,640]{1,0:T(8,128)(2,1)S(1)}, u32[]{:S(2)}, u32[]{:S(2)}) collective-permute-start(bf16[72,640]{1,0:T(8,128)(2,1)S(1)} %maximum_add_fusion.2), channel_id=1, source_target_pairs={{0,256},{16,272},{32,288},{48,304},{64,320},{80,336},{96,352},{112... | collective-permute-start | bytes 276488 | tf_op jit(solution)/shard_map/ppermute | solution.py:55
  29.5 4.3 %collective-permute-start.1 = (bf16[72,1152]{1,0:T(8,128)(2,1)}, bf16[72,1152]{1,0:T(8,128)(2,1)}, u32[]{:S(2)}, u32[]{:S(2)}) collective-permute-start(bf16[72,1152]{1,0:T(8,128)(2,1)} %collective-permute-done), channel_id=1, source_target_pairs={{0,32},{16,240},{32,64},{48,16},{64,96},{80,48},{96,128},{112,80},... | collective-permute-start | bytes 497672 | tf_op jit(solution)/shard_map/ppermute | solution.py:51
  33.8 4.3 %collective-permute-start.9 = (bf16[72,1152]{1,0:T(8,128)(2,1)S(1)}, bf16[72,1152]{1,0:T(8,128)(2,1)}, u32[]{:S(2)}, u32[]{:S(2)}) collective-permute-start(bf16[72,1152]{1,0:T(8,128)(2,1)S(1)} %collective-permute-done.8), channel_id=1, source_target_pairs={{0,32},{16,240},{32,64},{48,16},{64,96},{80,48},{96,128},{112,80},... | collective-permute-start | bytes 497672 | tf_op jit(solution)/shard_map/ppermute | solution.py:51
  38.3 1.6 bitcast_dynamic-update-slice_fusion.18
  41.8 5.2 %collective-permute-start.2 = (bf16[72,1152]{1,0:T(8,128)(2,1)}, bf16[72,1152]{1,0:T(8,128)(2,1)S(1)}, u32[]{:S(2)}, u32[]{:S(2)}) collective-permute-start(bf16[72,1152]{1,0:T(8,128)(2,1)} %collective-permute-done.1), channel_id=1, source_target_pairs={{0,32},{16,240},{32,64},{48,16},{64,96},{80,48},{96,128},{112,80},... | collective-permute-start | bytes 497672 | tf_op jit(solution)/shard_map/ppermute | solution.py:51
  46.9 3.4 %collective-permute-start.10 = (bf16[72,1152]{1,0:T(8,128)(2,1)}, bf16[72,1152]{1,0:T(8,128)(2,1)S(1)}, u32[]{:S(2)}, u32[]{:S(2)}) collective-permute-start(bf16[72,1152]{1,0:T(8,128)(2,1)} %collective-permute-done.9), channel_id=1, source_target_pairs={{0,32},{16,240},{32,64},{48,16},{64,96},{80,48},{96,128},{112,80},... | collective-permute-start | bytes 497672 | tf_op jit(solution)/shard_map/ppermute | solution.py:51
  51.3 1.6 bitcast_dynamic-update-slice_fusion.17
  52.9 3.4 %collective-permute-start.3 = (bf16[72,1152]{1,0:T(8,128)(2,1)S(1)}, bf16[72,1152]{1,0:T(8,128)(2,1)S(1)}, u32[]{:S(2)}, u32[]{:S(2)}) collective-permute-start(bf16[72,1152]{1,0:T(8,128)(2,1)S(1)} %collective-permute-done.2), channel_id=1, source_target_pairs={{0,32},{16,240},{32,64},{48,16},{64,96},{80,48},{96,128},{112,80},... | collective-permute-start | bytes 497672 | tf_op jit(solution)/shard_map/ppermute | solution.py:51
  56.3 3.4 %collective-permute-start.11 = (bf16[72,1152]{1,0:T(8,128)(2,1)S(1)}, bf16[72,1152]{1,0:T(8,128)(2,1)S(1)}, u32[]{:S(2)}, u32[]{:S(2)}) collective-permute-start(bf16[72,1152]{1,0:T(8,128)(2,1)S(1)} %collective-permute-done.10), channel_id=1, source_target_pairs={{0,32},{16,240},{32,64},{48,16},{64,96},{80,48},{96,128},{112,80},... | collective-permute-start | bytes 497672 | tf_op jit(solution)/shard_map/ppermute | solution.py:51
  61.4 4.2 %collective-permute-start.4 = (bf16[72,1152]{1,0:T(8,128)(2,1)S(1)}, bf16[72,1152]{1,0:T(8,128)(2,1)S(1)}, u32[]{:S(2)}, u32[]{:S(2)}) collective-permute-start(bf16[72,1152]{1,0:T(8,128)(2,1)S(1)} %collective-permute-done.3), channel_id=1, source_target_pairs={{0,32},{16,240},{32,64},{48,16},{64,96},{80,48},{96,128},{112,80},... | collective-permute-start | bytes 497672 | tf_op jit(solution)/shard_map/ppermute | solution.py:51
  66.5 3.6 %collective-permute-start.12 = (bf16[72,1152]{1,0:T(8,128)(2,1)S(1)}, bf16[72,1152]{1,0:T(8,128)(2,1)S(1)}, u32[]{:S(2)}, u32[]{:S(2)}) collective-permute-start(bf16[72,1152]{1,0:T(8,128)(2,1)S(1)} %collective-permute-done.11), channel_id=1, source_target_pairs={{0,32},{16,240},{32,64},{48,16},{64,96},{80,48},{96,128},{112,80},... | collective-permute-start | bytes 497672 | tf_op jit(solution)/shard_map/ppermute | solution.py:51
  71.8 2.8 collective-permute-start.5
  74.6 2.9 collective-permute-done.12
  77.5 1.9 collective-permute-start.13
  80.2 1.7 collective-permute-done.5
  81.9 2.6 collective-permute-start.6
  84.5 2.3 collective-permute-done.13
  86.8 1.9 collective-permute-start.14
  91.1 1.9 collective-permute-start.7
  99.0 3.3 %collective-permute-start.15 = (bf16[72,1152]{1,0:T(8,128)(2,1)}, bf16[72,1152]{1,0:T(8,128)(2,1)S(1)}, u32[]{:S(2)}, u32[]{:S(2)}) collective-permute-start(bf16[72,1152]{1,0:T(8,128)(2,1)} %collective-permute-done.14), channel_id=1, source_target_pairs={{0,32},{16,240},{32,64},{48,16},{64,96},{80,48},{96,128},{112,80},... | collective-permute-start | bytes 497672 | tf_op jit(solution)/shard_map/ppermute | solution.py:51
  103.2 4.4 %collective-permute-done.15 = bf16[72,1152]{1,0:T(8,128)(2,1)S(1)} collective-permute-done((bf16[72,1152]{1,0:T(8,128)(2,1)}, bf16[72,1152]{1,0:T(8,128)(2,1)S(1)}, u32[]{:S(2)}, u32[]{:S(2)}) %collective-permute-start.15) | collective-permute-done | bytes 165920 | tf_op jit(solution)/shard_map/ppermute | solution.py:51
  107.6 1.9 collective-permute-start.16
  112.0 1.9 copy.121
  113.9 2.4 collective-permute-start.18
  116.3 2.0 pad_maximum_fusion
  118.3 1.6 pad_maximum_fusion.1
  126.2 3.3 %collective-permute-start.19 = (bf16[64,1152]{1,0:T(8,128)(2,1)S(1)}, bf16[64,1152]{1,0:T(8,128)(2,1)S(1)}, u32[]{:S(2)}, u32[]{:S(2)}) collective-permute-start(bf16[64,1152]{1,0:T(8,128)(2,1)S(1)} %get-tuple-element.21), channel_id=1, source_target_pairs={{0,1},{1,2},{2,3},{3,0},{4,5},{5,6},{6,7},{7,4},{8,9},{9,10},{10,1... | collective-permute-start | bytes 442376 | tf_op jit(solution)/shard_map/ppermute | solution.py:105
  129.4 4.0 %collective-permute-start.21 = (bf16[64,1152]{1,0:T(8,128)(2,1)S(1)}, bf16[64,1152]{1,0:T(8,128)(2,1)S(1)}, u32[]{:S(2)}, u32[]{:S(2)}) collective-permute-start(bf16[64,1152]{1,0:T(8,128)(2,1)S(1)} %get-tuple-element.22), channel_id=1, source_target_pairs={{0,3},{1,0},{2,1},{3,2},{4,7},{5,4},{6,5},{7,6},{8,11},{9,8},{10,9... | collective-permute-start | bytes 442376 | tf_op jit(solution)/shard_map/ppermute | solution.py:105
  133.5 2.1 collective-permute-start.31
  135.6 5.0 %collective-permute-start.33 = (bf16[64,1152]{1,0:T(8,128)(2,1)S(1)}, bf16[64,1152]{1,0:T(8,128)(2,1)S(1)}, u32[]{:S(2)}, u32[]{:S(2)}) collective-permute-start(bf16[64,1152]{1,0:T(8,128)(2,1)S(1)} %get-tuple-element.20), channel_id=1, source_target_pairs={{0,3},{1,0},{2,1},{3,2},{4,7},{5,4},{6,5},{7,6},{8,11},{9,8},{10,9... | collective-permute-start | bytes 442376 | tf_op jit(solution)/shard_map/ppermute | solution.py:105
  140.8 1.9 collective-permute-start.20
  142.8 5.1 %collective-permute-start.22 = (bf16[64,2304]{1,0:T(8,128)(2,1)S(1)}, bf16[64,2304]{1,0:T(8,128)(2,1)S(1)}, u32[]{:S(2)}, u32[]{:S(2)}) collective-permute-start(bf16[64,2304]{1,0:T(8,128)(2,1)S(1)} %pad_maximum_fusion.7), channel_id=1, source_target_pairs={{0,3},{1,0},{2,1},{3,2},{4,7},{5,4},{6,5},{7,6},{8,11},{9,8},{10,9... | collective-permute-start | bytes 884744 | tf_op jit(solution)/shard_map/ppermute | solution.py:105
  148.0 1.9 collective-permute-start.32
  150.1 5.1 %collective-permute-start.34 = (bf16[64,2304]{1,0:T(8,128)(2,1)S(1)}, bf16[64,2304]{1,0:T(8,128)(2,1)S(1)}, u32[]{:S(2)}, u32[]{:S(2)}) collective-permute-start(bf16[64,2304]{1,0:T(8,128)(2,1)S(1)} %pad_maximum_fusion.9), channel_id=1, source_target_pairs={{0,3},{1,0},{2,1},{3,2},{4,7},{5,4},{6,5},{7,6},{8,11},{9,8},{10,9... | collective-permute-start | bytes 884744 | tf_op jit(solution)/shard_map/ppermute | solution.py:105
  155.4 3.4 %collective-permute-start.23 = (bf16[2,16,2304]{2,1,0:T(8,128)(2,1)S(1)}, bf16[2,16,2304]{2,1,0:T(8,128)(2,1)S(1)}, u32[]{:S(2)}, u32[]{:S(2)}) collective-permute-start(bf16[2,16,2304]{2,1,0:T(8,128)(2,1)S(1)} %fusion.43), channel_id=1, source_target_pairs={{0,4},{1,5},{2,6},{3,7},{4,0},{5,1},{6,2},{7,3},{8,12},{9,13},{10,... | collective-permute-start | bytes 442376 | tf_op jit(solution)/shard_map/ppermute | solution.py:59
  159.8 3.5 %collective-permute-start.35 = (bf16[2,16,2304]{2,1,0:T(8,128)(2,1)S(1)}, bf16[2,16,2304]{2,1,0:T(8,128)(2,1)S(1)}, u32[]{:S(2)}, u32[]{:S(2)}) collective-permute-start(bf16[2,16,2304]{2,1,0:T(8,128)(2,1)S(1)} %fusion.44), channel_id=1, source_target_pairs={{0,4},{1,5},{2,6},{3,7},{4,0},{5,1},{6,2},{7,3},{8,12},{9,13},{10,... | collective-permute-start | bytes 442376 | tf_op jit(solution)/shard_map/ppermute | solution.py:59
  163.5 3.8 %collective-permute-start.24 = (bf16[16,2304]{1,0:T(8,128)(2,1)S(1)}, bf16[16,2304]{1,0:T(8,128)(2,1)S(1)}, u32[]{:S(2)}, u32[]{:S(2)}) collective-permute-start(bf16[16,2304]{1,0:T(8,128)(2,1)S(1)} %fusion.59), channel_id=1, source_target_pairs={{0,8},{1,9},{2,10},{3,11},{4,12},{5,13},{6,14},{7,15},{8,0},{9,1},... | collective-permute-start | bytes 221192 | tf_op jit(solution)/shard_map/ppermute | solution.py:59
  167.8 3.2 %collective-permute-start.36 = (bf16[16,2304]{1,0:T(8,128)(2,1)S(1)}, bf16[16,2304]{1,0:T(8,128)(2,1)S(1)}, u32[]{:S(2)}, u32[]{:S(2)}) collective-permute-start(bf16[16,2304]{1,0:T(8,128)(2,1)S(1)} %fusion.60), channel_id=1, source_target_pairs={{0,8},{1,9},{2,10},{3,11},{4,12},{5,13},{6,14},{7,15},{8,0},{9,1},... | collective-permute-start | bytes 221192 | tf_op jit(solution)/shard_map/ppermute | solution.py:59
  172.4 3.4 %collective-permute-done.36 = bf16[16,2304]{1,0:T(8,128)(2,1)S(1)} collective-permute-done((bf16[16,2304]{1,0:T(8,128)(2,1)S(1)}, bf16[16,2304]{1,0:T(8,128)(2,1)S(1)}, u32[]{:S(2)}, u32[]{:S(2)}) %collective-permute-start.36) | collective-permute-done | bytes 73760 | tf_op jit(solution)/shard_map/ppermute | solution.py:59
  175.9 2.4 collective-permute-start.37
  178.3 4.3 %collective-permute-start.25 = (bf16[16,2304]{1,0:T(8,128)(2,1)S(1)}, bf16[16,2304]{1,0:T(8,128)(2,1)S(1)}, u32[]{:S(2)}, u32[]{:S(2)}) collective-permute-start(bf16[16,2304]{1,0:T(8,128)(2,1)S(1)} %get-tuple-element.26), channel_id=1, source_target_pairs={{0,8},{1,9},{2,10},{3,11},{4,12},{5,13},{6,14},{7,15},{8,0},{9,1},... | collective-permute-start | bytes 221192 | tf_op jit(solution)/shard_map/ppermute | solution.py:59
  182.7 2.1 collective-permute-done.37
  185.7 1.9 collective-permute-start.38
  187.7 3.9 %collective-permute-start.26 = (bf16[2,16,2304]{2,1,0:T(8,128)(2,1)S(1)}, bf16[2,16,2304]{2,1,0:T(8,128)(2,1)S(1)}, u32[]{:S(2)}, u32[]{:S(2)}) collective-permute-start(bf16[2,16,2304]{2,1,0:T(8,128)(2,1)S(1)} %maximum_select_fusion.3), channel_id=1, source_target_pairs={{0,4},{1,5},{2,6},{3,7},{4,0},{5,1},{6,2},{7,3},{8,12},{9,13},{10,... | collective-permute-start | bytes 442376 | tf_op jit(solution)/shard_map/ppermute | solution.py:59
  192.8 1.9 collective-permute-start.39
  194.7 5.1 %collective-permute-start.40 = (bf16[64,2304]{1,0:T(8,128)(2,1)S(1)}, bf16[64,2304]{1,0:T(8,128)(2,1)S(1)}, u32[]{:S(2)}, u32[]{:S(2)}) collective-permute-start(bf16[64,2304]{1,0:T(8,128)(2,1)S(1)} %bitcast.236), channel_id=1, source_target_pairs={{0,3},{1,0},{2,1},{3,2},{4,7},{5,4},{6,5},{7,6},{8,11},{9,8},{10,9... | collective-permute-start | bytes 884744 | tf_op jit(solution)/shard_map/ppermute | solution.py:105
  200.0 1.9 collective-permute-start.27
  201.9 5.1 %collective-permute-start.28 = (bf16[64,2304]{1,0:T(8,128)(2,1)S(1)}, bf16[64,2304]{1,0:T(8,128)(2,1)S(1)}, u32[]{:S(2)}, u32[]{:S(2)}) collective-permute-start(bf16[64,2304]{1,0:T(8,128)(2,1)S(1)} %bitcast.239), channel_id=1, source_target_pairs={{0,3},{1,0},{2,1},{3,2},{4,7},{5,4},{6,5},{7,6},{8,11},{9,8},{10,9... | collective-permute-start | bytes 884744 | tf_op jit(solution)/shard_map/ppermute | solution.py:105
  207.3 1.9 collective-permute-start.41
  209.3 5.1 %collective-permute-start.42 = (bf16[64,1152]{1,0:T(8,128)(2,1)S(1)}, bf16[64,1152]{1,0:T(8,128)(2,1)S(1)}, u32[]{:S(2)}, u32[]{:S(2)}) collective-permute-start(bf16[64,1152]{1,0:T(8,128)(2,1)S(1)} %slice.211), channel_id=1, source_target_pairs={{0,3},{1,0},{2,1},{3,2},{4,7},{5,4},{6,5},{7,6},{8,11},{9,8},{10,9... | collective-permute-start | bytes 442376 | tf_op jit(solution)/shard_map/ppermute | solution.py:105
  214.4 1.9 collective-permute-start.29
  216.4 5.1 %collective-permute-start.30 = (bf16[64,1152]{1,0:T(8,128)(2,1)S(1)}, bf16[64,1152]{1,0:T(8,128)(2,1)S(1)}, u32[]{:S(2)}, u32[]{:S(2)}) collective-permute-start(bf16[64,1152]{1,0:T(8,128)(2,1)S(1)} %slice.202), channel_id=1, source_target_pairs={{0,3},{1,0},{2,1},{3,2},{4,7},{5,4},{6,5},{7,6},{8,11},{9,8},{10,9... | collective-permute-start | bytes 442376 | tf_op jit(solution)/shard_map/ppermute | solution.py:105
  222.7 1.5 collective-permute-done.30
  226.4 2.5 fusion.39
  231.9 1.9 collective-permute-start.44
  235.0 2.4 collective-permute-start.43
  237.7 1.9 collective-permute-done.43
  241.3 6.2 %all-to-all-start = ((bf16[8,72,1152]{2,1,0:T(8,128)(2,1)}), bf16[8,72,1152]{2,1,0:T(8,128)(2,1)S(1)}, u32[]{:S(2)}, u32[]{:S(2)}) async-start(bf16[8,72,1152]{2,1,0:T(8,128)(2,1)} %pad_maximum_fusion.2), calls=%async_computation | async-start | bytes 2654208 | tf_op jit(solution)/shard_map/all_to_all | solution.py:76
  248.8 34.8 %all-to-all-done = bf16[8,72,1152]{2,1,0:T(8,128)(2,1)S(1)} async-done(((bf16[8,72,1152]{2,1,0:T(8,128)(2,1)}), bf16[8,72,1152]{2,1,0:T(8,128)(2,1)S(1)}, u32[]{:S(2)}, u32[]{:S(2)}) %all-to-all-start) | async-done | bytes 1327136 | tf_op jit(solution)/shard_map/all_to_all | solution.py:76
  283.9 5.0 %collective-permute-start.45 = (bf16[72,864]{1,0:T(8,128)(2,1)S(1)}, bf16[72,864]{1,0:T(8,128)(2,1)S(1)}, u32[]{:S(2)}, u32[]{:S(2)}) collective-permute-start(bf16[72,864]{1,0:T(8,128)(2,1)S(1)} %slice.319), channel_id=1, source_target_pairs={{0,256},{16,272},{32,288},{48,304},{64,320},{80,336},{96,352},{112... | collective-permute-start | bytes 373256 | tf_op jit(solution)/shard_map/ppermute | solution.py:55
  288.9 10.2 %reduce-scatter.4.cloned.1.call-done = bf16[1,72,576]{2,1,0:T(8,128)(2,1)} async-done(((bf16[8,72,576]{2,1,0:T(8,128)(2,1)}), bf16[1,72,576]{2,1,0:T(8,128)(2,1)}) %reduce-scatter.4.cloned.1.call-update) | async-done | bytes 82960
  301.0 1.7 fusion.56
  (204 shorter events, 51.9 us)
Async XLA Ops:
  7.2 13.6 %copy-start = (bf16[256,2304]{1,0:T(8,128)(2,1)S(1)}, bf16[256,2304]{1,0:T(8,128)(2,1)}, u32[]{:S(2)}) copy-start(bf16[256,2304]{1,0:T(8,128)(2,1)} %param.14) | copy-start | bytes 3538948
  7.2 13.6 %copy-start.17 = (s32[256]{0:T(256)S(1)}, s32[256]{0:T(256)}, u32[]{:S(2)}) copy-start(s32[256]{0:T(256)} %param.15) | copy-start | bytes 3076
  7.2 14.3 %copy-start.7 = (bf16[256,2304]{1,0:T(8,128)(2,1)S(1)}, bf16[256,2304]{1,0:T(8,128)(2,1)}, u32[]{:S(2)}) copy-start(bf16[256,2304]{1,0:T(8,128)(2,1)} %param.13) | copy-start | bytes 3538948
  7.2 104.8 %all-gather.3.cloned.1.call-start = ((), (), s32[]{:S(2)}) async-start(), calls=%async_computation.2 | async-start | bytes 1658880 | tf_op jit(solution)/shard_map/all_gather | solution.py:68
  8.4 14.4 %collective-permute-start = (bf16[72,1152]{1,0:T(8,128)(2,1)S(1)}, bf16[72,1152]{1,0:T(8,128)(2,1)}, u32[]{:S(2)}, u32[]{:S(2)}) collective-permute-start(bf16[72,1152]{1,0:T(8,128)(2,1)S(1)} %concatenate.79), channel_id=1, source_target_pairs={{0,32},{16,240},{32,64},{48,16},{64,96},{80,48},{96,128},{112,80},... | collective-permute-start | bytes 497672 | tf_op jit(solution)/shard_map/ppermute | solution.py:51
  12.7 21.1 %collective-permute-start.8 = (bf16[72,1152]{1,0:T(8,128)(2,1)S(1)}, bf16[72,1152]{1,0:T(8,128)(2,1)S(1)}, u32[]{:S(2)}, u32[]{:S(2)}) collective-permute-start(bf16[72,1152]{1,0:T(8,128)(2,1)S(1)} %concatenate.79), channel_id=1, source_target_pairs={{0,256},{16,272},{32,288},{48,304},{64,320},{80,336},{96,352},{112... | collective-permute-start | bytes 497672 | tf_op jit(solution)/shard_map/ppermute | solution.py:55
  21.5 3.2 %copy-start.10 = (bf16[288,72]{0,1:T(8,128)(2,1)S(1)}, bf16[288,72]{0,1:T(8,128)(2,1)}, u32[]{:S(2)}) copy-start(bf16[288,72]{0,1:T(8,128)(2,1)} %param.22) | copy-start | bytes 124420
  21.5 3.2 %copy-start.11 = (bf16[288,72]{0,1:T(8,128)(2,1)S(1)}, bf16[288,72]{0,1:T(8,128)(2,1)}, u32[]{:S(2)}) copy-start(bf16[288,72]{0,1:T(8,128)(2,1)} %param.19) | copy-start | bytes 124420
  24.8 15.9 %collective-permute-start.17 = (bf16[72,640]{1,0:T(8,128)(2,1)S(1)}, bf16[72,640]{1,0:T(8,128)(2,1)S(1)}, u32[]{:S(2)}, u32[]{:S(2)}) collective-permute-start(bf16[72,640]{1,0:T(8,128)(2,1)S(1)} %maximum_add_fusion.2), channel_id=1, source_target_pairs={{0,256},{16,272},{32,288},{48,304},{64,320},{80,336},{96,352},{112... | collective-permute-start | bytes 276488 | tf_op jit(solution)/shard_map/ppermute | solution.py:55
  29.5 12.2 %collective-permute-start.1 = (bf16[72,1152]{1,0:T(8,128)(2,1)}, bf16[72,1152]{1,0:T(8,128)(2,1)}, u32[]{:S(2)}, u32[]{:S(2)}) collective-permute-start(bf16[72,1152]{1,0:T(8,128)(2,1)} %collective-permute-done), channel_id=1, source_target_pairs={{0,32},{16,240},{32,64},{48,16},{64,96},{80,48},{96,128},{112,80},... | collective-permute-start | bytes 497672 | tf_op jit(solution)/shard_map/ppermute | solution.py:51
  33.8 13.1 %collective-permute-start.9 = (bf16[72,1152]{1,0:T(8,128)(2,1)S(1)}, bf16[72,1152]{1,0:T(8,128)(2,1)}, u32[]{:S(2)}, u32[]{:S(2)}) collective-permute-start(bf16[72,1152]{1,0:T(8,128)(2,1)S(1)} %collective-permute-done.8), channel_id=1, source_target_pairs={{0,32},{16,240},{32,64},{48,16},{64,96},{80,48},{96,128},{112,80},... | collective-permute-start | bytes 497672 | tf_op jit(solution)/shard_map/ppermute | solution.py:51
  41.8 11.1 %collective-permute-start.2 = (bf16[72,1152]{1,0:T(8,128)(2,1)}, bf16[72,1152]{1,0:T(8,128)(2,1)S(1)}, u32[]{:S(2)}, u32[]{:S(2)}) collective-permute-start(bf16[72,1152]{1,0:T(8,128)(2,1)} %collective-permute-done.1), channel_id=1, source_target_pairs={{0,32},{16,240},{32,64},{48,16},{64,96},{80,48},{96,128},{112,80},... | collective-permute-start | bytes 497672 | tf_op jit(solution)/shard_map/ppermute | solution.py:51
  46.9 9.3 %collective-permute-start.10 = (bf16[72,1152]{1,0:T(8,128)(2,1)}, bf16[72,1152]{1,0:T(8,128)(2,1)S(1)}, u32[]{:S(2)}, u32[]{:S(2)}) collective-permute-start(bf16[72,1152]{1,0:T(8,128)(2,1)} %collective-permute-done.9), channel_id=1, source_target_pairs={{0,32},{16,240},{32,64},{48,16},{64,96},{80,48},{96,128},{112,80},... | collective-permute-start | bytes 497672 | tf_op jit(solution)/shard_map/ppermute | solution.py:51
  52.9 8.5 %collective-permute-start.3 = (bf16[72,1152]{1,0:T(8,128)(2,1)S(1)}, bf16[72,1152]{1,0:T(8,128)(2,1)S(1)}, u32[]{:S(2)}, u32[]{:S(2)}) collective-permute-start(bf16[72,1152]{1,0:T(8,128)(2,1)S(1)} %collective-permute-done.2), channel_id=1, source_target_pairs={{0,32},{16,240},{32,64},{48,16},{64,96},{80,48},{96,128},{112,80},... | collective-permute-start | bytes 497672 | tf_op jit(solution)/shard_map/ppermute | solution.py:51
  56.3 10.2 %collective-permute-start.11 = (bf16[72,1152]{1,0:T(8,128)(2,1)S(1)}, bf16[72,1152]{1,0:T(8,128)(2,1)S(1)}, u32[]{:S(2)}, u32[]{:S(2)}) collective-permute-start(bf16[72,1152]{1,0:T(8,128)(2,1)S(1)} %collective-permute-done.10), channel_id=1, source_target_pairs={{0,32},{16,240},{32,64},{48,16},{64,96},{80,48},{96,128},{112,80},... | collective-permute-start | bytes 497672 | tf_op jit(solution)/shard_map/ppermute | solution.py:51
  61.4 10.4 %collective-permute-start.4 = (bf16[72,1152]{1,0:T(8,128)(2,1)S(1)}, bf16[72,1152]{1,0:T(8,128)(2,1)S(1)}, u32[]{:S(2)}, u32[]{:S(2)}) collective-permute-start(bf16[72,1152]{1,0:T(8,128)(2,1)S(1)} %collective-permute-done.3), channel_id=1, source_target_pairs={{0,32},{16,240},{32,64},{48,16},{64,96},{80,48},{96,128},{112,80},... | collective-permute-start | bytes 497672 | tf_op jit(solution)/shard_map/ppermute | solution.py:51
  66.5 11.0 %collective-permute-start.12 = (bf16[72,1152]{1,0:T(8,128)(2,1)S(1)}, bf16[72,1152]{1,0:T(8,128)(2,1)S(1)}, u32[]{:S(2)}, u32[]{:S(2)}) collective-permute-start(bf16[72,1152]{1,0:T(8,128)(2,1)S(1)} %collective-permute-done.11), channel_id=1, source_target_pairs={{0,32},{16,240},{32,64},{48,16},{64,96},{80,48},{96,128},{112,80},... | collective-permute-start | bytes 497672 | tf_op jit(solution)/shard_map/ppermute | solution.py:51
  71.8 10.1 %collective-permute-start.5 = (bf16[72,1152]{1,0:T(8,128)(2,1)S(1)}, bf16[72,1152]{1,0:T(8,128)(2,1)S(1)}, u32[]{:S(2)}, u32[]{:S(2)}) collective-permute-start(bf16[72,1152]{1,0:T(8,128)(2,1)S(1)} %collective-permute-done.4), channel_id=1, source_target_pairs={{0,32},{16,240},{32,64},{48,16},{64,96},{80,48},{96,128},{112,80},... | collective-permute-start | bytes 497672 | tf_op jit(solution)/shard_map/ppermute | solution.py:51
  77.5 9.3 %collective-permute-start.13 = (bf16[72,1152]{1,0:T(8,128)(2,1)S(1)}, bf16[72,1152]{1,0:T(8,128)(2,1)}, u32[]{:S(2)}, u32[]{:S(2)}) collective-permute-start(bf16[72,1152]{1,0:T(8,128)(2,1)S(1)} %collective-permute-done.12), channel_id=1, source_target_pairs={{0,32},{16,240},{32,64},{48,16},{64,96},{80,48},{96,128},{112,80},... | collective-permute-start | bytes 497672 | tf_op jit(solution)/shard_map/ppermute | solution.py:51
  81.9 8.5 %collective-permute-start.6 = (bf16[72,1152]{1,0:T(8,128)(2,1)S(1)}, bf16[72,1152]{1,0:T(8,128)(2,1)S(1)}, u32[]{:S(2)}, u32[]{:S(2)}) collective-permute-start(bf16[72,1152]{1,0:T(8,128)(2,1)S(1)} %collective-permute-done.5), channel_id=1, source_target_pairs={{0,32},{16,240},{32,64},{48,16},{64,96},{80,48},{96,128},{112,80},... | collective-permute-start | bytes 497672 | tf_op jit(solution)/shard_map/ppermute | solution.py:51
  86.8 12.1 %collective-permute-start.14 = (bf16[72,1152]{1,0:T(8,128)(2,1)}, bf16[72,1152]{1,0:T(8,128)(2,1)}, u32[]{:S(2)}, u32[]{:S(2)}) collective-permute-start(bf16[72,1152]{1,0:T(8,128)(2,1)} %collective-permute-done.13), channel_id=1, source_target_pairs={{0,32},{16,240},{32,64},{48,16},{64,96},{80,48},{96,128},{112,80},... | collective-permute-start | bytes 497672 | tf_op jit(solution)/shard_map/ppermute | solution.py:51
  91.1 25.2 %collective-permute-start.7 = (bf16[8,72,1152]{2,1,0:T(8,128)(2,1)}, bf16[8,72,1152]{2,1,0:T(8,128)(2,1)}, u32[]{:S(2)}, u32[]{:S(2)}) collective-permute-start(bf16[8,72,1152]{2,1,0:T(8,128)(2,1)} %bitcast_dynamic-update-slice_fusion.12), channel_id=1, source_target_pairs={{0,16},{16,0},{32,48},{48,32},{64,80},{80,64},{96,112},{112,96},{1... | collective-permute-start | bytes 3981320 | tf_op jit(solution)/shard_map/ppermute | solution.py:55
  96.9 1.6 copy-start.6
  99.0 8.7 %collective-permute-start.15 = (bf16[72,1152]{1,0:T(8,128)(2,1)}, bf16[72,1152]{1,0:T(8,128)(2,1)S(1)}, u32[]{:S(2)}, u32[]{:S(2)}) collective-permute-start(bf16[72,1152]{1,0:T(8,128)(2,1)} %collective-permute-done.14), channel_id=1, source_target_pairs={{0,32},{16,240},{32,64},{48,16},{64,96},{80,48},{96,128},{112,80},... | collective-permute-start | bytes 497672 | tf_op jit(solution)/shard_map/ppermute | solution.py:51
  107.6 10.7 %collective-permute-start.16 = (bf16[8,72,1152]{2,1,0:T(8,128)(2,1)S(1)}, bf16[8,72,1152]{2,1,0:T(8,128)(2,1)}, u32[]{:S(2)}, u32[]{:S(2)}) collective-permute-start(bf16[8,72,1152]{2,1,0:T(8,128)(2,1)S(1)} %bitcast_dynamic-update-slice_fusion.4), channel_id=1, source_target_pairs={{0,16},{16,0},{32,48},{48,32},{64,80},{80,64},{96,112},{112,96},{1... | collective-permute-start | bytes 3981320 | tf_op jit(solution)/shard_map/ppermute | solution.py:55
  111.9 9.0 %copy-start.2 = (bf16[2,2,256,576]{2,3,1,0:T(8,128)(2,1)}, bf16[2,2,256,576]{2,3,1,0:T(8,128)(2,1)S(1)}, u32[]{:S(2)}) copy-start(bf16[2,2,256,576]{2,3,1,0:T(8,128)(2,1)S(1)} %reverse_select_fusion) | copy-start | bytes 3538948
  113.9 8.6 %collective-permute-start.18 = (bf16[8,2,72,640]{3,2,0,1:T(8,128)(2,1)S(1)}, bf16[8,2,72,640]{3,2,0,1:T(8,128)(2,1)S(1)}, u32[]{:S(2)}, u32[]{:S(2)}) collective-permute-start(bf16[8,2,72,640]{3,2,0,1:T(8,128)(2,1)S(1)} %copy.121), channel_id=1, source_target_pairs={{0,16},{16,0},{32,48},{48,32},{64,80},{80,64},{96,112},{112,96},{1... | collective-permute-start | bytes 4423688 | tf_op jit(solution)/shard_map/ppermute | solution.py:55
  122.0 1.8 copy-start.5
  126.2 14.6 %collective-permute-start.19 = (bf16[64,1152]{1,0:T(8,128)(2,1)S(1)}, bf16[64,1152]{1,0:T(8,128)(2,1)S(1)}, u32[]{:S(2)}, u32[]{:S(2)}) collective-permute-start(bf16[64,1152]{1,0:T(8,128)(2,1)S(1)} %get-tuple-element.21), channel_id=1, source_target_pairs={{0,1},{1,2},{2,3},{3,0},{4,5},{5,6},{6,7},{7,4},{8,9},{9,10},{10,1... | collective-permute-start | bytes 442376 | tf_op jit(solution)/shard_map/ppermute | solution.py:105
  129.4 13.3 %collective-permute-start.21 = (bf16[64,1152]{1,0:T(8,128)(2,1)S(1)}, bf16[64,1152]{1,0:T(8,128)(2,1)S(1)}, u32[]{:S(2)}, u32[]{:S(2)}) collective-permute-start(bf16[64,1152]{1,0:T(8,128)(2,1)S(1)} %get-tuple-element.22), channel_id=1, source_target_pairs={{0,3},{1,0},{2,1},{3,2},{4,7},{5,4},{6,5},{7,6},{8,11},{9,8},{10,9... | collective-permute-start | bytes 442376 | tf_op jit(solution)/shard_map/ppermute | solution.py:105
  133.5 14.5 %collective-permute-start.31 = (bf16[64,1152]{1,0:T(8,128)(2,1)S(1)}, bf16[64,1152]{1,0:T(8,128)(2,1)S(1)}, u32[]{:S(2)}, u32[]{:S(2)}) collective-permute-start(bf16[64,1152]{1,0:T(8,128)(2,1)S(1)} %get-tuple-element.19), channel_id=1, source_target_pairs={{0,1},{1,2},{2,3},{3,0},{4,5},{5,6},{6,7},{7,4},{8,9},{9,10},{10,1... | collective-permute-start | bytes 442376 | tf_op jit(solution)/shard_map/ppermute | solution.py:105
  135.6 14.4 %collective-permute-start.33 = (bf16[64,1152]{1,0:T(8,128)(2,1)S(1)}, bf16[64,1152]{1,0:T(8,128)(2,1)S(1)}, u32[]{:S(2)}, u32[]{:S(2)}) collective-permute-start(bf16[64,1152]{1,0:T(8,128)(2,1)S(1)} %get-tuple-element.20), channel_id=1, source_target_pairs={{0,3},{1,0},{2,1},{3,2},{4,7},{5,4},{6,5},{7,6},{8,11},{9,8},{10,9... | collective-permute-start | bytes 442376 | tf_op jit(solution)/shard_map/ppermute | solution.py:105
  140.8 14.4 %collective-permute-start.20 = (bf16[64,2304]{1,0:T(8,128)(2,1)S(1)}, bf16[64,2304]{1,0:T(8,128)(2,1)S(1)}, u32[]{:S(2)}, u32[]{:S(2)}) collective-permute-start(bf16[64,2304]{1,0:T(8,128)(2,1)S(1)} %pad_maximum_fusion.6), channel_id=1, source_target_pairs={{0,1},{1,2},{2,3},{3,0},{4,5},{5,6},{6,7},{7,4},{8,9},{9,10},{10,1... | collective-permute-start | bytes 884744 | tf_op jit(solution)/shard_map/ppermute | solution.py:105
  142.8 12.4 %collective-permute-start.22 = (bf16[64,2304]{1,0:T(8,128)(2,1)S(1)}, bf16[64,2304]{1,0:T(8,128)(2,1)S(1)}, u32[]{:S(2)}, u32[]{:S(2)}) collective-permute-start(bf16[64,2304]{1,0:T(8,128)(2,1)S(1)} %pad_maximum_fusion.7), channel_id=1, source_target_pairs={{0,3},{1,0},{2,1},{3,2},{4,7},{5,4},{6,5},{7,6},{8,11},{9,8},{10,9... | collective-permute-start | bytes 884744 | tf_op jit(solution)/shard_map/ppermute | solution.py:105
  148.0 10.7 %collective-permute-start.32 = (bf16[64,2304]{1,0:T(8,128)(2,1)S(1)}, bf16[64,2304]{1,0:T(8,128)(2,1)S(1)}, u32[]{:S(2)}, u32[]{:S(2)}) collective-permute-start(bf16[64,2304]{1,0:T(8,128)(2,1)S(1)} %pad_maximum_fusion.8), channel_id=1, source_target_pairs={{0,1},{1,2},{2,3},{3,0},{4,5},{5,6},{6,7},{7,4},{8,9},{9,10},{10,1... | collective-permute-start | bytes 884744 | tf_op jit(solution)/shard_map/ppermute | solution.py:105
  150.1 9.6 %collective-permute-start.34 = (bf16[64,2304]{1,0:T(8,128)(2,1)S(1)}, bf16[64,2304]{1,0:T(8,128)(2,1)S(1)}, u32[]{:S(2)}, u32[]{:S(2)}) collective-permute-start(bf16[64,2304]{1,0:T(8,128)(2,1)S(1)} %pad_maximum_fusion.9), channel_id=1, source_target_pairs={{0,3},{1,0},{2,1},{3,2},{4,7},{5,4},{6,5},{7,6},{8,11},{9,8},{10,9... | collective-permute-start | bytes 884744 | tf_op jit(solution)/shard_map/ppermute | solution.py:105
  155.4 8.1 %collective-permute-start.23 = (bf16[2,16,2304]{2,1,0:T(8,128)(2,1)S(1)}, bf16[2,16,2304]{2,1,0:T(8,128)(2,1)S(1)}, u32[]{:S(2)}, u32[]{:S(2)}) collective-permute-start(bf16[2,16,2304]{2,1,0:T(8,128)(2,1)S(1)} %fusion.43), channel_id=1, source_target_pairs={{0,4},{1,5},{2,6},{3,7},{4,0},{5,1},{6,2},{7,3},{8,12},{9,13},{10,... | collective-permute-start | bytes 442376 | tf_op jit(solution)/shard_map/ppermute | solution.py:59
  159.8 11.3 %copy-start.15 = (f32[256,32]{0,1:T(8,128)S(1)}, f32[256,32]{0,1:T(8,128)}, u32[]{:S(2)}) copy-start(f32[256,32]{0,1:T(8,128)} %fusion.61) | copy-start | bytes 98308
  159.8 16.0 %copy-start.8 = (f32[16,2304]{1,0:T(8,128)S(1)}, f32[16,2304]{1,0:T(8,128)}, u32[]{:S(2)}) copy-start(f32[16,2304]{1,0:T(8,128)} %reshape.330) | copy-start | bytes 442372
  159.8 16.0 %copy-start.9 = (f32[16,2304]{1,0:T(8,128)S(1)}, f32[16,2304]{1,0:T(8,128)}, u32[]{:S(2)}) copy-start(f32[16,2304]{1,0:T(8,128)} %reshape.332) | copy-start | bytes 442372
  159.8 8.0 %collective-permute-start.35 = (bf16[2,16,2304]{2,1,0:T(8,128)(2,1)S(1)}, bf16[2,16,2304]{2,1,0:T(8,128)(2,1)S(1)}, u32[]{:S(2)}, u32[]{:S(2)}) collective-permute-start(bf16[2,16,2304]{2,1,0:T(8,128)(2,1)S(1)} %fusion.44), channel_id=1, source_target_pairs={{0,4},{1,5},{2,6},{3,7},{4,0},{5,1},{6,2},{7,3},{8,12},{9,13},{10,... | collective-permute-start | bytes 442376 | tf_op jit(solution)/shard_map/ppermute | solution.py:59
  163.5 8.9 %collective-permute-start.24 = (bf16[16,2304]{1,0:T(8,128)(2,1)S(1)}, bf16[16,2304]{1,0:T(8,128)(2,1)S(1)}, u32[]{:S(2)}, u32[]{:S(2)}) collective-permute-start(bf16[16,2304]{1,0:T(8,128)(2,1)S(1)} %fusion.59), channel_id=1, source_target_pairs={{0,8},{1,9},{2,10},{3,11},{4,12},{5,13},{6,14},{7,15},{8,0},{9,1},... | collective-permute-start | bytes 221192 | tf_op jit(solution)/shard_map/ppermute | solution.py:59
  167.8 7.9 %collective-permute-start.36 = (bf16[16,2304]{1,0:T(8,128)(2,1)S(1)}, bf16[16,2304]{1,0:T(8,128)(2,1)S(1)}, u32[]{:S(2)}, u32[]{:S(2)}) collective-permute-start(bf16[16,2304]{1,0:T(8,128)(2,1)S(1)} %fusion.60), channel_id=1, source_target_pairs={{0,8},{1,9},{2,10},{3,11},{4,12},{5,13},{6,14},{7,15},{8,0},{9,1},... | collective-permute-start | bytes 221192 | tf_op jit(solution)/shard_map/ppermute | solution.py:59
  175.9 8.8 %collective-permute-start.37 = (bf16[16,2304]{1,0:T(8,128)(2,1)S(1)}, bf16[16,2304]{1,0:T(8,128)(2,1)}, u32[]{:S(2)}, u32[]{:S(2)}) collective-permute-start(bf16[16,2304]{1,0:T(8,128)(2,1)S(1)} %get-tuple-element.25), channel_id=1, source_target_pairs={{0,8},{1,9},{2,10},{3,11},{4,12},{5,13},{6,14},{7,15},{8,0},{9,1},... | collective-permute-start | bytes 221192 | tf_op jit(solution)/shard_map/ppermute | solution.py:59
  178.3 9.3 %collective-permute-start.25 = (bf16[16,2304]{1,0:T(8,128)(2,1)S(1)}, bf16[16,2304]{1,0:T(8,128)(2,1)S(1)}, u32[]{:S(2)}, u32[]{:S(2)}) collective-permute-start(bf16[16,2304]{1,0:T(8,128)(2,1)S(1)} %get-tuple-element.26), channel_id=1, source_target_pairs={{0,8},{1,9},{2,10},{3,11},{4,12},{5,13},{6,14},{7,15},{8,0},{9,1},... | collective-permute-start | bytes 221192 | tf_op jit(solution)/shard_map/ppermute | solution.py:59
  185.7 7.0 %collective-permute-start.38 = (bf16[2,16,2304]{2,1,0:T(8,128)(2,1)S(1)}, bf16[2,16,2304]{2,1,0:T(8,128)(2,1)S(1)}, u32[]{:S(2)}, u32[]{:S(2)}) collective-permute-start(bf16[2,16,2304]{2,1,0:T(8,128)(2,1)S(1)} %maximum_select_fusion.4), channel_id=1, source_target_pairs={{0,4},{1,5},{2,6},{3,7},{4,0},{5,1},{6,2},{7,3},{8,12},{9,13},{10,... | collective-permute-start | bytes 442376 | tf_op jit(solution)/shard_map/ppermute | solution.py:59
  187.7 12.2 %collective-permute-start.26 = (bf16[2,16,2304]{2,1,0:T(8,128)(2,1)S(1)}, bf16[2,16,2304]{2,1,0:T(8,128)(2,1)S(1)}, u32[]{:S(2)}, u32[]{:S(2)}) collective-permute-start(bf16[2,16,2304]{2,1,0:T(8,128)(2,1)S(1)} %maximum_select_fusion.3), channel_id=1, source_target_pairs={{0,4},{1,5},{2,6},{3,7},{4,0},{5,1},{6,2},{7,3},{8,12},{9,13},{10,... | collective-permute-start | bytes 442376 | tf_op jit(solution)/shard_map/ppermute | solution.py:59
  192.8 14.5 %collective-permute-start.39 = (bf16[64,2304]{1,0:T(8,128)(2,1)S(1)}, bf16[64,2304]{1,0:T(8,128)(2,1)S(1)}, u32[]{:S(2)}, u32[]{:S(2)}) collective-permute-start(bf16[64,2304]{1,0:T(8,128)(2,1)S(1)} %bitcast.235), channel_id=1, source_target_pairs={{0,1},{1,2},{2,3},{3,0},{4,5},{5,6},{6,7},{7,4},{8,9},{9,10},{10,1... | collective-permute-start | bytes 884744 | tf_op jit(solution)/shard_map/ppermute | solution.py:105
  194.7 14.5 %collective-permute-start.40 = (bf16[64,2304]{1,0:T(8,128)(2,1)S(1)}, bf16[64,2304]{1,0:T(8,128)(2,1)S(1)}, u32[]{:S(2)}, u32[]{:S(2)}) collective-permute-start(bf16[64,2304]{1,0:T(8,128)(2,1)S(1)} %bitcast.236), channel_id=1, source_target_pairs={{0,3},{1,0},{2,1},{3,2},{4,7},{5,4},{6,5},{7,6},{8,11},{9,8},{10,9... | collective-permute-start | bytes 884744 | tf_op jit(solution)/shard_map/ppermute | solution.py:105
  200.0 14.4 %collective-permute-start.27 = (bf16[64,2304]{1,0:T(8,128)(2,1)S(1)}, bf16[64,2304]{1,0:T(8,128)(2,1)S(1)}, u32[]{:S(2)}, u32[]{:S(2)}) collective-permute-start(bf16[64,2304]{1,0:T(8,128)(2,1)S(1)} %bitcast.238), channel_id=1, source_target_pairs={{0,1},{1,2},{2,3},{3,0},{4,5},{5,6},{6,7},{7,4},{8,9},{9,10},{10,1... | collective-permute-start | bytes 884744 | tf_op jit(solution)/shard_map/ppermute | solution.py:105
  201.9 14.5 %collective-permute-start.28 = (bf16[64,2304]{1,0:T(8,128)(2,1)S(1)}, bf16[64,2304]{1,0:T(8,128)(2,1)S(1)}, u32[]{:S(2)}, u32[]{:S(2)}) collective-permute-start(bf16[64,2304]{1,0:T(8,128)(2,1)S(1)} %bitcast.239), channel_id=1, source_target_pairs={{0,3},{1,0},{2,1},{3,2},{4,7},{5,4},{6,5},{7,6},{8,11},{9,8},{10,9... | collective-permute-start | bytes 884744 | tf_op jit(solution)/shard_map/ppermute | solution.py:105
  207.3 17.4 %collective-permute-start.41 = (bf16[64,1152]{1,0:T(8,128)(2,1)S(1)}, bf16[64,1152]{1,0:T(8,128)(2,1)S(1)}, u32[]{:S(2)}, u32[]{:S(2)}) collective-permute-start(bf16[64,1152]{1,0:T(8,128)(2,1)S(1)} %slice.210), channel_id=1, source_target_pairs={{0,1},{1,2},{2,3},{3,0},{4,5},{5,6},{6,7},{7,4},{8,9},{9,10},{10,1... | collective-permute-start | bytes 442376 | tf_op jit(solution)/shard_map/ppermute | solution.py:105
  209.3 16.0 %collective-permute-start.42 = (bf16[64,1152]{1,0:T(8,128)(2,1)S(1)}, bf16[64,1152]{1,0:T(8,128)(2,1)S(1)}, u32[]{:S(2)}, u32[]{:S(2)}) collective-permute-start(bf16[64,1152]{1,0:T(8,128)(2,1)S(1)} %slice.211), channel_id=1, source_target_pairs={{0,3},{1,0},{2,1},{3,2},{4,7},{5,4},{6,5},{7,6},{8,11},{9,8},{10,9... | collective-permute-start | bytes 442376 | tf_op jit(solution)/shard_map/ppermute | solution.py:105
  214.4 8.2 %collective-permute-start.29 = (bf16[64,1152]{1,0:T(8,128)(2,1)S(1)}, bf16[64,1152]{1,0:T(8,128)(2,1)S(1)}, u32[]{:S(2)}, u32[]{:S(2)}) collective-permute-start(bf16[64,1152]{1,0:T(8,128)(2,1)S(1)} %slice.201), channel_id=1, source_target_pairs={{0,1},{1,2},{2,3},{3,0},{4,5},{5,6},{6,7},{7,4},{8,9},{9,10},{10,1... | collective-permute-start | bytes 442376 | tf_op jit(solution)/shard_map/ppermute | solution.py:105
  216.4 7.8 %collective-permute-start.30 = (bf16[64,1152]{1,0:T(8,128)(2,1)S(1)}, bf16[64,1152]{1,0:T(8,128)(2,1)S(1)}, u32[]{:S(2)}, u32[]{:S(2)}) collective-permute-start(bf16[64,1152]{1,0:T(8,128)(2,1)S(1)} %slice.202), channel_id=1, source_target_pairs={{0,3},{1,0},{2,1},{3,2},{4,7},{5,4},{6,5},{7,6},{8,11},{9,8},{10,9... | collective-permute-start | bytes 442376 | tf_op jit(solution)/shard_map/ppermute | solution.py:105
  231.9 5.5 %collective-permute-start.44 = (bf16[8,72,864]{2,1,0:T(8,128)(2,1)S(1)}, bf16[8,72,864]{2,1,0:T(8,128)(2,1)S(1)}, u32[]{:S(2)}, u32[]{:S(2)}) collective-permute-start(bf16[8,72,864]{2,1,0:T(8,128)(2,1)S(1)} %bitcast.241), channel_id=1, source_target_pairs={{0,16},{16,0},{32,48},{48,32},{64,80},{80,64},{96,112},{112,96},{1... | collective-permute-start | bytes 2985992 | tf_op jit(solution)/shard_map/ppermute | solution.py:55
  235.0 4.7 %collective-permute-start.43 = (bf16[8,72,864]{2,1,0:T(8,128)(2,1)S(1)}, bf16[8,72,864]{2,1,0:T(8,128)(2,1)S(1)}, u32[]{:S(2)}, u32[]{:S(2)}) collective-permute-start(bf16[8,72,864]{2,1,0:T(8,128)(2,1)S(1)} %bitcast.242), channel_id=1, source_target_pairs={{0,16},{16,0},{32,48},{48,32},{64,80},{80,64},{96,112},{112,96},{1... | collective-permute-start | bytes 2985992 | tf_op jit(solution)/shard_map/ppermute | solution.py:55
  241.3 42.4 %all-to-all-start = ((bf16[8,72,1152]{2,1,0:T(8,128)(2,1)}), bf16[8,72,1152]{2,1,0:T(8,128)(2,1)S(1)}, u32[]{:S(2)}, u32[]{:S(2)}) async-start(bf16[8,72,1152]{2,1,0:T(8,128)(2,1)} %pad_maximum_fusion.2), calls=%async_computation | async-start | bytes 2654208 | tf_op jit(solution)/shard_map/all_to_all | solution.py:76
  247.5 51.7 %reduce-scatter.4.cloned.1.call-start = ((), (), s32[]{:S(2)}) async-start(), calls=%async_computation.3 | async-start | bytes 829440
  248.8 51.4 %copy-start.14 = (f32[288,72]{0,1:T(8,128)S(1)}, f32[288,72]{0,1:T(8,128)}, u32[]{:S(2)}) copy-start(f32[288,72]{0,1:T(8,128)} %param.25) | copy-start | bytes 248836
  248.8 52.2 %copy-start.12 = (bf16[72,288]{1,0:T(8,128)(2,1)S(1)}, bf16[72,288]{1,0:T(8,128)(2,1)}, u32[]{:S(2)}) copy-start(bf16[72,288]{1,0:T(8,128)(2,1)} %param.20) | copy-start | bytes 124420
  248.8 52.2 %copy-start.13 = (bf16[72,288]{1,0:T(8,128)(2,1)S(1)}, bf16[72,288]{1,0:T(8,128)(2,1)}, u32[]{:S(2)}) copy-start(bf16[72,288]{1,0:T(8,128)(2,1)} %param.21) | copy-start | bytes 124420
  283.7 19.0 %copy-start.1 = (bf16[256,2304]{1,0:T(8,128)(2,1)S(1)}, bf16[256,2304]{1,0:T(8,128)(2,1)}, u32[]{:S(2)}) copy-start(bf16[256,2304]{1,0:T(8,128)(2,1)} %param.14) | copy-start | bytes 3538948
  283.9 16.2 %collective-permute-start.45 = (bf16[72,864]{1,0:T(8,128)(2,1)S(1)}, bf16[72,864]{1,0:T(8,128)(2,1)S(1)}, u32[]{:S(2)}, u32[]{:S(2)}) collective-permute-start(bf16[72,864]{1,0:T(8,128)(2,1)S(1)} %slice.319), channel_id=1, source_target_pairs={{0,256},{16,272},{32,288},{48,304},{64,320},{80,336},{96,352},{112... | collective-permute-start | bytes 373256 | tf_op jit(solution)/shard_map/ppermute | solution.py:55
  (3 other events, 3.8 us)
Sparse Core Ops, SparseCore 0:
  41.5 45.3 all-gather.2
  251.1 47.9 reduce-scatter.3
where the time goes:
time: 312 us; the launch traced here: 310 us
  starting transfers between devices  163 us (52%)
  waiting for transfers between devices  72.8 us (23%)
  local copies, waits for them, and re-layouts  27.3 us (9%)
  other arithmetic  19 us (6%)
  between operations  16.9 us (5%)
  matrix products  10.9 us (3%)
    ppermute x16, starting transfers between devices, x_shift(): return lax.ppermute(array, 'tensor', perm)  56.6 us
    ppermute x14, starting transfers between devices, ring_step(): return lax.ppermute(array, 'seq', perm)  48.4 us
    all_to_all x1, waiting for transfers between devices, group_exchange(): return lax.all_to_all(array, axis, 0, 0, axis_index_groups=groups)  34.8 us
    ppermute x8, starting transfers between devices, y_swap(): return lax.ppermute(array, 'tensor', [(t, t ^ bit * 4) for t in range(16)])  26.4 us
    ppermute x8, starting transfers between devices, seq_swap(): return lax.ppermute(array, 'seq', [(s, s ^ bit) for s in range(32)])  25.1 us
    ppermute x14, waiting for transfers between devices, ring_step(): return lax.ppermute(array, 'seq', perm)  14.9 us
    dynamic_update_slice x16, local copies, waits for them, and re-layouts, in_order(): lax.dynamic_update_slice(own, chunk[None], ((z - sign * k) % NZ, 0, 0))  10.3 us
    unnamed x3, waiting for transfers between devices  10.2 us
  transfers between devices with their start and end apart: 49, of which 21 were waited for; matrix products, arithmetic and copies ran while one was open for 13% of the time, Pallas kernels for 0%

commit v1 on v0

--- a/solution.py
+++ b/solution.py
@@ -168,17 +168,14 @@
     def put(buf, piece, at, col=0):
         return lax.dynamic_update_slice(buf, piece[None], ((x + at) % 4, 0, col))
 
-    ups = [x_shift(r, 1) for r in rows]
-    downs = [x_shift(r, -1) for r in rows]
-    far_ups = [x_shift(up[:, :h], 1) for up in ups]
-    far_downs = [x_shift(down[:, h:], -1) for down in downs]
-    result = []
-    for own, up, down, far_up, far_down in zip(rows, ups, downs, far_ups, far_downs):
-        buf = put(jnp.zeros((4, 64, n), own.dtype), own, 0)
-        buf = put(put(buf, up, 3), down, 1)
-        buf = put(put(buf, far_up, 2), far_down, 2, h)
-        result.append(buf.reshape(256, n))
-    return result
+    own = rows[0]
+    up, down = x_shift(own, 1), x_shift(own, -1)
+    second = group_gather(rows[1], "tensor", X_GROUPS)
+    buf = put(jnp.zeros((4, 64, n), own.dtype), own, 0)
+    buf = put(put(buf, up, 3), down, 1)
+    buf = put(buf, x_shift(up[:, :h], 1), 2)
+    buf = put(buf, x_shift(down[:, h:], -1), 2, h)
+    return [buf.reshape(256, n), second.reshape(256, n)]
 
 
 def relative(rows, y, c):
@@ -217,17 +214,16 @@
     tally = jnp.pad(jnp.sum(onehot, axis=0).astype(BF)[None], ((0, ROWS - 1), (0, TALLY - 32)))
     own_out = jnp.concatenate([w_down.T, dir_down.T, tally], axis=1)
     across_in = seq_swap(own_in, 16)
-    near_held = ring_chunks(own_in)
-    near = in_order(near_held, z, sign)
-    own_out = after(own_out, near_held[1])
+    near = group_exchange(jnp.broadcast_to(own_in[None], (NZ,) + own_in.shape), "seq", Z_GROUPS)
     outs = group_gather(jnp.stack([own_out, seq_swap(own_out, 16)]), "seq", Z_GROUPS)
+    away_held = ring_chunks(across_in)
     near_other = seq_swap(near, 1)
-    away = in_order(ring_chunks(across_in), z, sign)
     outs_other = seq_swap(outs, 1)
+    away = in_order(away_held, z, sign)
     away_other = seq_swap(away, 1)
 
-    tokens = after(tokens, near_held[-1])
-    target = after(target, near_held[-1])
+    tokens = after(tokens, away_held[1])
+    target = after(target, away_held[2])
     wide = tokens.astype(F32)
     scale = lax.rsqrt(jnp.mean(wide * wide, axis=1, keepdims=True) + norm_eps)
     normed = (wide * scale * norm_gain).astype(BF)

time: 312 us -> 330 us (1.058)
  waiting for transfers between devices: 72.8 us -> 134 us
  starting transfers between devices: 163 us -> 124 us
  local copies, waits for them, and re-layouts: 27.3 us -> 20.6 us
    ppermute x14 -> x7, waiting for transfers between devices: 14.9 us -> 60.1 us  [ring_step(): return lax.ppermute(array, 'seq', perm)]
    ppermute x14 -> x7, starting transfers between devices: 48.4 us -> 15.3 us  [ring_step(): return lax.ppermute(array, 'seq', perm)]
    ppermute x16 -> x12, starting transfers between devices: 56.6 us -> 43 us  [x_shift(): return lax.ppermute(array, 'tensor', perm)]
    all_to_all x1 -> x2, starting transfers between devices: 6.18 us -> 17.9 us  [group_exchange(): return lax.all_to_all(array, axis, 0, 0, axis_index_groups=groups)]
    dynamic_update_slice x16 -> x8, local copies, waits for them, and re-layouts: 10.3 us -> 0.2 us  [in_order(): lax.dynamic_update_slice(own, chunk[None], ((z - sign * k) % NZ, 0, 0))]
    all_gather x1 -> x2, waiting for transfers between devices: 0.02 us -> 8.15 us  [group_gather(): return lax.all_gather(array, axis, axis_index_groups=groups)]
    ppermute x8, waiting for transfers between devices: 1.94 us -> 6.45 us  [seq_swap(): return lax.ppermute(array, 'seq', [(s, s ^ bit) for s in range(32)])]
    ppermute x8, starting transfers between devices: 26.4 us -> 22.1 us  [y_swap(): return lax.ppermute(array, 'tensor', [(t, t ^ bit * 4) for t in range(16)])]
  transfers between devices with their start and end apart: 49 -> 40, of which waited for: 21 -> 21; matrix products, arithmetic and copies ran while one was open for 13% -> 11% of each run, Pallas kernels for 0% -> 0%
where the time goes in v1:
time: 330 us; the launch traced here: 327 us
  waiting for transfers between devices  134 us (41%)
  starting transfers between devices  124 us (38%)
  local copies, waits for them, and re-layouts  20.6 us (6%)
  other arithmetic  19.5 us (6%)
  between operations  16.7 us (5%)
  matrix products  12.9 us (4%)
    ppermute x7, waiting for transfers between devices, ring_step(): return lax.ppermute(array, 'seq', perm)  60.1 us
    ppermute x12, starting transfers between devices, x_shift(): return lax.ppermute(array, 'tensor', perm)  43 us
    all_to_all x2, waiting for transfers between devices, group_exchange(): return lax.all_to_all(array, axis, 0, 0, axis_index_groups=groups)  35.7 us
    ppermute x8, starting transfers between devices, seq_swap(): return lax.ppermute(array, 'seq', [(s, s ^ bit) for s in range(32)])  25.4 us
    ppermute x8, starting transfers between devices, y_swap(): return lax.ppermute(array, 'tensor', [(t, t ^ bit * 4) for t in range(16)])  22.1 us
    all_to_all x2, starting transfers between devices, group_exchange(): return lax.all_to_all(array, axis, 0, 0, axis_index_groups=groups)  17.9 us
    ppermute x7, starting transfers between devices, ring_step(): return lax.ppermute(array, 'seq', perm)  15.3 us
    ppermute x8, waiting for transfers between devices, y_swap(): return lax.ppermute(array, 'tensor', [(t, t ^ bit * 4) for t in range(16)])  9.09 us
  transfers between devices with their start and end apart: 40, of which 21 were waited for; matrix products, arithmetic and copies ran while one was open for 11% of the time, Pallas kernels for 0%

profile of v1, /device:TPU:56, one launch (start us, length us, event | category | flops | bytes accessed | tf_op | source)
XLA Modules:
  0.0 327.2 jit_solution(13614265455933657695)
XLA Ops:
  8.2 4.7 %collective-permute-start = (bf16[72,1152]{1,0:T(8,128)(2,1)S(1)}, bf16[72,1152]{1,0:T(8,128)(2,1)S(1)}, u32[]{:S(2)}, u32[]{:S(2)}) collective-permute-start(bf16[72,1152]{1,0:T(8,128)(2,1)S(1)} %concatenate.64), channel_id=1, source_target_pairs={{0,256},{16,272},{32,288},{48,304},{64,320},{80,336},{96,352},{112... | collective-permute-start | bytes 497672 | tf_op jit(solution)/shard_map/ppermute | solution.py:55
  14.1 10.5 %all-to-all-start = ((bf16[8,72,1152]{2,1,0:T(8,128)(2,1)}), bf16[8,72,1152]{2,1,0:T(8,128)(2,1)}, u32[]{:S(2)}, u32[]{:S(2)}) async-start(bf16[8,72,1152]{2,1,0:T(8,128)(2,1)} %broadcast_in_dim.55), calls=%async_computation | async-start | bytes 2654208 | tf_op jit(solution)/shard_map/all_to_all | solution.py:76
  24.9 5.0 %collective-permute-start.10 = (bf16[72,640]{1,0:T(8,128)(2,1)S(1)}, bf16[72,640]{1,0:T(8,128)(2,1)S(1)}, u32[]{:S(2)}, u32[]{:S(2)}) collective-permute-start(bf16[72,640]{1,0:T(8,128)(2,1)S(1)} %fusion.60), channel_id=1, source_target_pairs={{0,256},{16,272},{32,288},{48,304},{64,320},{80,336},{96,352},{112... | collective-permute-start | bytes 276488 | tf_op jit(solution)/shard_map/ppermute | solution.py:55
  31.7 4.5 %collective-permute-done.10 = bf16[72,640]{1,0:T(8,128)(2,1)S(1)} collective-permute-done((bf16[72,640]{1,0:T(8,128)(2,1)S(1)}, bf16[72,640]{1,0:T(8,128)(2,1)S(1)}, u32[]{:S(2)}, u32[]{:S(2)}) %collective-permute-start.10) | collective-permute-done | bytes 92192 | tf_op jit(solution)/shard_map/ppermute | solution.py:55
  37.0 3.9 %collective-permute-start.1 = (bf16[72,1152]{1,0:T(8,128)(2,1)S(1)}, bf16[72,1152]{1,0:T(8,128)(2,1)S(1)}, u32[]{:S(2)}, u32[]{:S(2)}) collective-permute-start(bf16[72,1152]{1,0:T(8,128)(2,1)S(1)} %collective-permute-done), channel_id=1, source_target_pairs={{0,32},{16,240},{32,64},{48,16},{64,96},{80,48},{96,128},{112,80},... | collective-permute-start | bytes 497672 | tf_op jit(solution)/shard_map/ppermute | solution.py:51
  41.0 19.0 %collective-permute-done.1 = bf16[72,1152]{1,0:T(8,128)(2,1)S(1)} collective-permute-done((bf16[72,1152]{1,0:T(8,128)(2,1)S(1)}, bf16[72,1152]{1,0:T(8,128)(2,1)S(1)}, u32[]{:S(2)}, u32[]{:S(2)}) %collective-permute-start.1) | collective-permute-done | bytes 165920 | tf_op jit(solution)/shard_map/ppermute | solution.py:51
  62.0 1.9 collective-permute-start.3
  64.3 7.7 %collective-permute-done.3 = bf16[72,1152]{1,0:T(8,128)(2,1)S(1)} collective-permute-done((bf16[72,1152]{1,0:T(8,128)(2,1)S(1)}, bf16[72,1152]{1,0:T(8,128)(2,1)S(1)}, u32[]{:S(2)}, u32[]{:S(2)}) %collective-permute-start.3) | collective-permute-done | bytes 165920 | tf_op jit(solution)/shard_map/ppermute | solution.py:51
  72.0 1.9 collective-permute-start.4
  74.0 7.5 %collective-permute-done.4 = bf16[72,1152]{1,0:T(8,128)(2,1)S(1)} collective-permute-done((bf16[72,1152]{1,0:T(8,128)(2,1)S(1)}, bf16[72,1152]{1,0:T(8,128)(2,1)S(1)}, u32[]{:S(2)}, u32[]{:S(2)}) %collective-permute-start.4) | collective-permute-done | bytes 165920 | tf_op jit(solution)/shard_map/ppermute | solution.py:51
  81.5 1.9 collective-permute-start.5
  83.4 6.5 %collective-permute-done.5 = bf16[72,1152]{1,0:T(8,128)(2,1)S(1)} collective-permute-done((bf16[72,1152]{1,0:T(8,128)(2,1)S(1)}, bf16[72,1152]{1,0:T(8,128)(2,1)S(1)}, u32[]{:S(2)}, u32[]{:S(2)}) %collective-permute-start.5) | collective-permute-done | bytes 165920 | tf_op jit(solution)/shard_map/ppermute | solution.py:51
  89.9 1.9 collective-permute-start.6
  91.8 6.5 %collective-permute-done.6 = bf16[72,1152]{1,0:T(8,128)(2,1)S(1)} collective-permute-done((bf16[72,1152]{1,0:T(8,128)(2,1)S(1)}, bf16[72,1152]{1,0:T(8,128)(2,1)S(1)}, u32[]{:S(2)}, u32[]{:S(2)}) %collective-permute-start.6) | collective-permute-done | bytes 165920 | tf_op jit(solution)/shard_map/ppermute | solution.py:51
  98.3 1.9 collective-permute-start.7
  100.3 6.5 %collective-permute-done.7 = bf16[72,1152]{1,0:T(8,128)(2,1)S(1)} collective-permute-done((bf16[72,1152]{1,0:T(8,128)(2,1)S(1)}, bf16[72,1152]{1,0:T(8,128)(2,1)S(1)}, u32[]{:S(2)}, u32[]{:S(2)}) %collective-permute-start.7) | collective-permute-done | bytes 165920 | tf_op jit(solution)/shard_map/ppermute | solution.py:51
  106.8 1.9 collective-permute-start.8
  108.7 6.5 %collective-permute-done.8 = bf16[72,1152]{1,0:T(8,128)(2,1)S(1)} collective-permute-done((bf16[72,1152]{1,0:T(8,128)(2,1)S(1)}, bf16[72,1152]{1,0:T(8,128)(2,1)S(1)}, u32[]{:S(2)}, u32[]{:S(2)}) %collective-permute-start.8) | collective-permute-done | bytes 165920 | tf_op jit(solution)/shard_map/ppermute | solution.py:51
  115.2 1.9 collective-permute-start.9
  117.1 1.3 reverse_select_fusion.1
  118.9 2.1 reverse_select_fusion
  123.5 2.4 collective-permute-start.2
  127.8 1.5 copy.111
  129.3 1.9 collective-permute-start.11
  131.3 1.6 pad_maximum_fusion.1
  133.9 2.0 pad_maximum_fusion
  141.1 3.4 %collective-permute-start.12 = (bf16[64,1152]{1,0:T(8,128)(2,1)S(1)}, bf16[64,1152]{1,0:T(8,128)(2,1)S(1)}, u32[]{:S(2)}, u32[]{:S(2)}) collective-permute-start(bf16[64,1152]{1,0:T(8,128)(2,1)S(1)} %get-tuple-element.21), channel_id=1, source_target_pairs={{0,1},{1,2},{2,3},{3,0},{4,5},{5,6},{6,7},{7,4},{8,9},{9,10},{10,1... | collective-permute-start | bytes 442376 | tf_op jit(solution)/shard_map/ppermute | solution.py:105
  144.6 3.6 %collective-permute-start.14 = (bf16[64,1152]{1,0:T(8,128)(2,1)S(1)}, bf16[64,1152]{1,0:T(8,128)(2,1)S(1)}, u32[]{:S(2)}, u32[]{:S(2)}) collective-permute-start(bf16[64,1152]{1,0:T(8,128)(2,1)S(1)} %get-tuple-element.22), channel_id=1, source_target_pairs={{0,3},{1,0},{2,1},{3,2},{4,7},{5,4},{6,5},{7,6},{8,11},{9,8},{10,9... | collective-permute-start | bytes 442376 | tf_op jit(solution)/shard_map/ppermute | solution.py:105
  148.3 2.2 collective-permute-start.20
  150.5 4.8 %collective-permute-start.22 = (bf16[64,1152]{1,0:T(8,128)(2,1)S(1)}, bf16[64,1152]{1,0:T(8,128)(2,1)S(1)}, u32[]{:S(2)}, u32[]{:S(2)}) collective-permute-start(bf16[64,1152]{1,0:T(8,128)(2,1)S(1)} %get-tuple-element.20), channel_id=1, source_target_pairs={{0,3},{1,0},{2,1},{3,2},{4,7},{5,4},{6,5},{7,6},{8,11},{9,8},{10,9... | collective-permute-start | bytes 442376 | tf_op jit(solution)/shard_map/ppermute | solution.py:105
  155.6 1.9 collective-permute-start.13
  157.6 5.1 %collective-permute-start.15 = (bf16[64,2304]{1,0:T(8,128)(2,1)S(1)}, bf16[64,2304]{1,0:T(8,128)(2,1)S(1)}, u32[]{:S(2)}, u32[]{:S(2)}) collective-permute-start(bf16[64,2304]{1,0:T(8,128)(2,1)S(1)} %pad_maximum_fusion.7), channel_id=1, source_target_pairs={{0,3},{1,0},{2,1},{3,2},{4,7},{5,4},{6,5},{7,6},{8,11},{9,8},{10,9... | collective-permute-start | bytes 884744 | tf_op jit(solution)/shard_map/ppermute | solution.py:105
  162.8 2.1 collective-permute-start.21
  165.0 5.1 %collective-permute-start.23 = (bf16[64,2304]{1,0:T(8,128)(2,1)S(1)}, bf16[64,2304]{1,0:T(8,128)(2,1)S(1)}, u32[]{:S(2)}, u32[]{:S(2)}) collective-permute-start(bf16[64,2304]{1,0:T(8,128)(2,1)S(1)} %pad_maximum_fusion.9), channel_id=1, source_target_pairs={{0,3},{1,0},{2,1},{3,2},{4,7},{5,4},{6,5},{7,6},{8,11},{9,8},{10,9... | collective-permute-start | bytes 884744 | tf_op jit(solution)/shard_map/ppermute | solution.py:105
  170.3 2.6 collective-permute-start.16
  173.7 1.5 collective-permute-done.23
  175.3 2.8 collective-permute-start.24
  178.1 1.9 collective-permute-start.17
  180.1 3.2 collective-permute-done.24
  183.3 2.2 collective-permute-start.25
  185.6 1.9 collective-permute-done.17
  187.5 3.1 collective-permute-done.25
  190.7 2.1 collective-permute-start.26
  192.9 4.6 %collective-permute-start.18 = (bf16[16,2304]{1,0:T(8,128)(2,1)S(1)}, bf16[16,2304]{1,0:T(8,128)(2,1)S(1)}, u32[]{:S(2)}, u32[]{:S(2)}) collective-permute-start(bf16[16,2304]{1,0:T(8,128)(2,1)S(1)} %get-tuple-element.26), channel_id=1, source_target_pairs={{0,8},{1,9},{2,10},{3,11},{4,12},{5,13},{6,14},{7,15},{8,0},{9,1},... | collective-permute-start | bytes 221192 | tf_op jit(solution)/shard_map/ppermute | solution.py:59
  199.2 1.9 collective-permute-start.27
  201.2 3.9 %collective-permute-start.19 = (bf16[2,16,2304]{2,1,0:T(8,128)(2,1)S(1)}, bf16[2,16,2304]{2,1,0:T(8,128)(2,1)S(1)}, u32[]{:S(2)}, u32[]{:S(2)}) collective-permute-start(bf16[2,16,2304]{2,1,0:T(8,128)(2,1)S(1)} %maximum_select_fusion.3), channel_id=1, source_target_pairs={{0,4},{1,5},{2,6},{3,7},{4,0},{5,1},{6,2},{7,3},{8,12},{9,13},{10,... | collective-permute-start | bytes 442376 | tf_op jit(solution)/shard_map/ppermute | solution.py:59
  207.0 1.9 collective-permute-start.28
  209.0 5.6 %collective-permute-start.29 = (bf16[64,2304]{1,0:T(8,128)(2,1)}, bf16[64,2304]{1,0:T(8,128)(2,1)}, u32[]{:S(2)}, u32[]{:S(2)}) collective-permute-start(bf16[64,2304]{1,0:T(8,128)(2,1)} %bitcast.72), channel_id=1, source_target_pairs={{0,3},{1,0},{2,1},{3,2},{4,7},{5,4},{6,5},{7,6},{8,11},{9,8},{10,9... | collective-permute-start | bytes 884744 | tf_op jit(solution)/shard_map/ppermute | solution.py:105
  218.6 1.9 collective-permute-start.30
  221.4 5.1 %collective-permute-start.31 = (bf16[64,1152]{1,0:T(8,128)(2,1)S(1)}, bf16[64,1152]{1,0:T(8,128)(2,1)S(1)}, u32[]{:S(2)}, u32[]{:S(2)}) collective-permute-start(bf16[64,1152]{1,0:T(8,128)(2,1)S(1)} %slice.200), channel_id=1, source_target_pairs={{0,3},{1,0},{2,1},{3,2},{4,7},{5,4},{6,5},{7,6},{8,11},{9,8},{10,9... | collective-permute-start | bytes 442376 | tf_op jit(solution)/shard_map/ppermute | solution.py:105
  228.6 2.5 collective-permute-done.31
  232.2 1.9 fusion.71
  234.1 8.2 %all-gather.4.cloned.1.call-done = bf16[4,64,2304]{2,1,0:T(8,128)(2,1)} async-done(((bf16[1,64,2304]{2,1,0:T(8,128)(2,1)}), bf16[4,64,2304]{2,1,0:T(8,128)(2,1)}) %all-gather.4.cloned.1.call-update) | async-done | bytes 1179664 | tf_op jit(solution)/shard_map/all_gather | solution.py:68
  242.3 1.7 fusion.18
  245.0 2.6 fusion.39
  250.6 1.9 collective-permute-start.33
  253.7 2.4 collective-permute-start.32
  256.4 1.9 collective-permute-done.32
  258.6 1.4 pad_maximum_fusion.2
  260.0 7.4 %all-to-all-start.1 = ((bf16[8,72,1152]{2,1,0:T(8,128)(2,1)}), bf16[8,72,1152]{2,1,0:T(8,128)(2,1)S(1)}, u32[]{:S(2)}, u32[]{:S(2)}) async-start(bf16[8,72,1152]{2,1,0:T(8,128)(2,1)} %pad_maximum_fusion.2), calls=%async_computation.1 | async-start | bytes 2654208 | tf_op jit(solution)/shard_map/all_to_all | solution.py:76
  267.4 1.3 slice.213
  268.8 35.7 %all-to-all-done.1 = bf16[8,72,1152]{2,1,0:T(8,128)(2,1)S(1)} async-done(((bf16[8,72,1152]{2,1,0:T(8,128)(2,1)}), bf16[8,72,1152]{2,1,0:T(8,128)(2,1)S(1)}, u32[]{:S(2)}, u32[]{:S(2)}) %all-to-all-start.1) | async-done | bytes 1327136 | tf_op jit(solution)/shard_map/all_to_all | solution.py:76
  304.7 5.1 %collective-permute-start.34 = (bf16[72,864]{1,0:T(8,128)(2,1)S(1)}, bf16[72,864]{1,0:T(8,128)(2,1)S(1)}, u32[]{:S(2)}, u32[]{:S(2)}) collective-permute-start(bf16[72,864]{1,0:T(8,128)(2,1)S(1)} %slice.308), channel_id=1, source_target_pairs={{0,256},{16,272},{32,288},{48,304},{64,320},{80,336},{96,352},{112... | collective-permute-start | bytes 373256 | tf_op jit(solution)/shard_map/ppermute | solution.py:55
  309.8 8.2 %reduce-scatter.4.cloned.1.call-done = bf16[1,72,576]{2,1,0:T(8,128)(2,1)} async-done(((bf16[8,72,576]{2,1,0:T(8,128)(2,1)}), bf16[1,72,576]{2,1,0:T(8,128)(2,1)}) %reduce-scatter.4.cloned.1.call-update) | async-done | bytes 82960
  (174 shorter events, 38.8 us)
Async XLA Ops:
  8.2 28.8 %collective-permute-start = (bf16[72,1152]{1,0:T(8,128)(2,1)S(1)}, bf16[72,1152]{1,0:T(8,128)(2,1)S(1)}, u32[]{:S(2)}, u32[]{:S(2)}) collective-permute-start(bf16[72,1152]{1,0:T(8,128)(2,1)S(1)} %concatenate.64), channel_id=1, source_target_pairs={{0,256},{16,272},{32,288},{48,304},{64,320},{80,336},{96,352},{112... | collective-permute-start | bytes 497672 | tf_op jit(solution)/shard_map/ppermute | solution.py:55
  14.1 10.5 %copy-start.19 = (s32[256]{0:T(256)S(1)}, s32[256]{0:T(256)}, u32[]{:S(2)}) copy-start(s32[256]{0:T(256)} %param.15) | copy-start | bytes 3076
  14.1 10.6 %copy-start.10 = (bf16[288,72]{0,1:T(8,128)(2,1)S(1)}, bf16[288,72]{0,1:T(8,128)(2,1)}, u32[]{:S(2)}) copy-start(bf16[288,72]{0,1:T(8,128)(2,1)} %param.22) | copy-start | bytes 124420
  14.1 10.6 %copy-start.13 = (bf16[288,72]{0,1:T(8,128)(2,1)S(1)}, bf16[288,72]{0,1:T(8,128)(2,1)}, u32[]{:S(2)}) copy-start(bf16[288,72]{0,1:T(8,128)(2,1)} %param.19) | copy-start | bytes 124420
  14.1 16.8 %copy-start.7 = (bf16[256,2304]{1,0:T(8,128)(2,1)S(1)}, bf16[256,2304]{1,0:T(8,128)(2,1)}, u32[]{:S(2)}) copy-start(bf16[256,2304]{1,0:T(8,128)(2,1)} %param.13) | copy-start | bytes 3538948
  14.1 109.4 %all-to-all-start = ((bf16[8,72,1152]{2,1,0:T(8,128)(2,1)}), bf16[8,72,1152]{2,1,0:T(8,128)(2,1)}, u32[]{:S(2)}, u32[]{:S(2)}) async-start(bf16[8,72,1152]{2,1,0:T(8,128)(2,1)} %broadcast_in_dim.55), calls=%async_computation | async-start | bytes 2654208 | tf_op jit(solution)/shard_map/all_to_all | solution.py:76
  24.6 103.2 %all-gather.6.cloned.1.call-start = ((), (), s32[]{:S(2)}) async-start(), calls=%async_computation.4 | async-start | bytes 1658880 | tf_op jit(solution)/shard_map/all_gather | solution.py:68
  24.9 11.3 %collective-permute-start.10 = (bf16[72,640]{1,0:T(8,128)(2,1)S(1)}, bf16[72,640]{1,0:T(8,128)(2,1)S(1)}, u32[]{:S(2)}, u32[]{:S(2)}) collective-permute-start(bf16[72,640]{1,0:T(8,128)(2,1)S(1)} %fusion.60), channel_id=1, source_target_pairs={{0,256},{16,272},{32,288},{48,304},{64,320},{80,336},{96,352},{112... | collective-permute-start | bytes 276488 | tf_op jit(solution)/shard_map/ppermute | solution.py:55
  36.9 205.3 %all-gather.4.cloned.1.call-start = ((), (), s32[]{:S(2)}) async-start(), calls=%async_computation.3 | async-start | bytes 1474560 | tf_op jit(solution)/shard_map/all_gather | solution.py:68
  37.0 23.0 %collective-permute-start.1 = (bf16[72,1152]{1,0:T(8,128)(2,1)S(1)}, bf16[72,1152]{1,0:T(8,128)(2,1)S(1)}, u32[]{:S(2)}, u32[]{:S(2)}) collective-permute-start(bf16[72,1152]{1,0:T(8,128)(2,1)S(1)} %collective-permute-done), channel_id=1, source_target_pairs={{0,32},{16,240},{32,64},{48,16},{64,96},{80,48},{96,128},{112,80},... | collective-permute-start | bytes 497672 | tf_op jit(solution)/shard_map/ppermute | solution.py:51
  41.0 20.7 %copy-start.18 = (f32[2304]{0:T(1024)S(1)}, f32[2304]{0:T(1024)}, u32[]{:S(2)}) copy-start(f32[2304]{0:T(1024)} %param.16) | copy-start | bytes 27652
  62.0 10.0 %collective-permute-start.3 = (bf16[72,1152]{1,0:T(8,128)(2,1)S(1)}, bf16[72,1152]{1,0:T(8,128)(2,1)S(1)}, u32[]{:S(2)}, u32[]{:S(2)}) collective-permute-start(bf16[72,1152]{1,0:T(8,128)(2,1)S(1)} %collective-permute-done.1), channel_id=1, source_target_pairs={{0,32},{16,240},{32,64},{48,16},{64,96},{80,48},{96,128},{112,80},... | collective-permute-start | bytes 497672 | tf_op jit(solution)/shard_map/ppermute | solution.py:51
  72.0 9.4 %collective-permute-start.4 = (bf16[72,1152]{1,0:T(8,128)(2,1)S(1)}, bf16[72,1152]{1,0:T(8,128)(2,1)S(1)}, u32[]{:S(2)}, u32[]{:S(2)}) collective-permute-start(bf16[72,1152]{1,0:T(8,128)(2,1)S(1)} %collective-permute-done.3), channel_id=1, source_target_pairs={{0,32},{16,240},{32,64},{48,16},{64,96},{80,48},{96,128},{112,80},... | collective-permute-start | bytes 497672 | tf_op jit(solution)/shard_map/ppermute | solution.py:51
  81.5 8.4 %collective-permute-start.5 = (bf16[72,1152]{1,0:T(8,128)(2,1)S(1)}, bf16[72,1152]{1,0:T(8,128)(2,1)S(1)}, u32[]{:S(2)}, u32[]{:S(2)}) collective-permute-start(bf16[72,1152]{1,0:T(8,128)(2,1)S(1)} %collective-permute-done.4), channel_id=1, source_target_pairs={{0,32},{16,240},{32,64},{48,16},{64,96},{80,48},{96,128},{112,80},... | collective-permute-start | bytes 497672 | tf_op jit(solution)/shard_map/ppermute | solution.py:51
  89.9 8.4 %collective-permute-start.6 = (bf16[72,1152]{1,0:T(8,128)(2,1)S(1)}, bf16[72,1152]{1,0:T(8,128)(2,1)S(1)}, u32[]{:S(2)}, u32[]{:S(2)}) collective-permute-start(bf16[72,1152]{1,0:T(8,128)(2,1)S(1)} %collective-permute-done.5), channel_id=1, source_target_pairs={{0,32},{16,240},{32,64},{48,16},{64,96},{80,48},{96,128},{112,80},... | collective-permute-start | bytes 497672 | tf_op jit(solution)/shard_map/ppermute | solution.py:51
  98.3 8.4 %collective-permute-start.7 = (bf16[72,1152]{1,0:T(8,128)(2,1)S(1)}, bf16[72,1152]{1,0:T(8,128)(2,1)S(1)}, u32[]{:S(2)}, u32[]{:S(2)}) collective-permute-start(bf16[72,1152]{1,0:T(8,128)(2,1)S(1)} %collective-permute-done.6), channel_id=1, source_target_pairs={{0,32},{16,240},{32,64},{48,16},{64,96},{80,48},{96,128},{112,80},... | collective-permute-start | bytes 497672 | tf_op jit(solution)/shard_map/ppermute | solution.py:51
  106.8 8.4 %collective-permute-start.8 = (bf16[72,1152]{1,0:T(8,128)(2,1)S(1)}, bf16[72,1152]{1,0:T(8,128)(2,1)S(1)}, u32[]{:S(2)}, u32[]{:S(2)}) collective-permute-start(bf16[72,1152]{1,0:T(8,128)(2,1)S(1)} %collective-permute-done.7), channel_id=1, source_target_pairs={{0,32},{16,240},{32,64},{48,16},{64,96},{80,48},{96,128},{112,80},... | collective-permute-start | bytes 497672 | tf_op jit(solution)/shard_map/ppermute | solution.py:51
  115.2 16.1 %collective-permute-start.9 = (bf16[8,72,1152]{2,1,0:T(8,128)(2,1)S(1)}, bf16[8,72,1152]{2,1,0:T(8,128)(2,1)}, u32[]{:S(2)}, u32[]{:S(2)}) collective-permute-start(bf16[8,72,1152]{2,1,0:T(8,128)(2,1)S(1)} %bitcast_dynamic-update-slice_fusion.2), channel_id=1, source_target_pairs={{0,16},{16,0},{32,48},{48,32},{64,80},{80,64},{96,112},{112,96},{1... | collective-permute-start | bytes 3981320 | tf_op jit(solution)/shard_map/ppermute | solution.py:55
  120.9 15.0 %copy-start = (bf16[2,2,256,576]{2,3,1,0:T(8,128)(2,1)}, bf16[2,2,256,576]{2,3,1,0:T(8,128)(2,1)S(1)}, u32[]{:S(2)}) copy-start(bf16[2,2,256,576]{2,3,1,0:T(8,128)(2,1)S(1)} %reverse_select_fusion) | copy-start | bytes 3538948
  123.5 10.4 %collective-permute-start.2 = (bf16[8,72,1152]{2,1,0:T(8,128)(2,1)}, bf16[8,72,1152]{2,1,0:T(8,128)(2,1)}, u32[]{:S(2)}, u32[]{:S(2)}) collective-permute-start(bf16[8,72,1152]{2,1,0:T(8,128)(2,1)} %all-to-all-done), channel_id=1, source_target_pairs={{0,16},{16,0},{32,48},{48,32},{64,80},{80,64},{96,112},{112,96},{1... | collective-permute-start | bytes 3981320 | tf_op jit(solution)/shard_map/ppermute | solution.py:55
  129.3 8.1 %collective-permute-start.11 = (bf16[8,2,72,640]{3,2,0,1:T(8,128)(2,1)S(1)}, bf16[8,2,72,640]{3,2,0,1:T(8,128)(2,1)S(1)}, u32[]{:S(2)}, u32[]{:S(2)}) collective-permute-start(bf16[8,2,72,640]{3,2,0,1:T(8,128)(2,1)S(1)} %copy.111), channel_id=1, source_target_pairs={{0,16},{16,0},{32,48},{48,32},{64,80},{80,64},{96,112},{112,96},{1... | collective-permute-start | bytes 4423688 | tf_op jit(solution)/shard_map/ppermute | solution.py:55
  137.0 1.0 copy-start.2
  137.0 1.8 copy-start.3
  141.1 14.4 %collective-permute-start.12 = (bf16[64,1152]{1,0:T(8,128)(2,1)S(1)}, bf16[64,1152]{1,0:T(8,128)(2,1)S(1)}, u32[]{:S(2)}, u32[]{:S(2)}) collective-permute-start(bf16[64,1152]{1,0:T(8,128)(2,1)S(1)} %get-tuple-element.21), channel_id=1, source_target_pairs={{0,1},{1,2},{2,3},{3,0},{4,5},{5,6},{6,7},{7,4},{8,9},{9,10},{10,1... | collective-permute-start | bytes 442376 | tf_op jit(solution)/shard_map/ppermute | solution.py:105
  144.6 13.0 %collective-permute-start.14 = (bf16[64,1152]{1,0:T(8,128)(2,1)S(1)}, bf16[64,1152]{1,0:T(8,128)(2,1)S(1)}, u32[]{:S(2)}, u32[]{:S(2)}) collective-permute-start(bf16[64,1152]{1,0:T(8,128)(2,1)S(1)} %get-tuple-element.22), channel_id=1, source_target_pairs={{0,3},{1,0},{2,1},{3,2},{4,7},{5,4},{6,5},{7,6},{8,11},{9,8},{10,9... | collective-permute-start | bytes 442376 | tf_op jit(solution)/shard_map/ppermute | solution.py:105
  148.3 14.5 %collective-permute-start.20 = (bf16[64,1152]{1,0:T(8,128)(2,1)S(1)}, bf16[64,1152]{1,0:T(8,128)(2,1)S(1)}, u32[]{:S(2)}, u32[]{:S(2)}) collective-permute-start(bf16[64,1152]{1,0:T(8,128)(2,1)S(1)} %get-tuple-element.19), channel_id=1, source_target_pairs={{0,1},{1,2},{2,3},{3,0},{4,5},{5,6},{6,7},{7,4},{8,9},{9,10},{10,1... | collective-permute-start | bytes 442376 | tf_op jit(solution)/shard_map/ppermute | solution.py:105
  150.5 14.4 %collective-permute-start.22 = (bf16[64,1152]{1,0:T(8,128)(2,1)S(1)}, bf16[64,1152]{1,0:T(8,128)(2,1)S(1)}, u32[]{:S(2)}, u32[]{:S(2)}) collective-permute-start(bf16[64,1152]{1,0:T(8,128)(2,1)S(1)} %get-tuple-element.20), channel_id=1, source_target_pairs={{0,3},{1,0},{2,1},{3,2},{4,7},{5,4},{6,5},{7,6},{8,11},{9,8},{10,9... | collective-permute-start | bytes 442376 | tf_op jit(solution)/shard_map/ppermute | solution.py:105
  155.6 14.6 %collective-permute-start.13 = (bf16[64,2304]{1,0:T(8,128)(2,1)S(1)}, bf16[64,2304]{1,0:T(8,128)(2,1)S(1)}, u32[]{:S(2)}, u32[]{:S(2)}) collective-permute-start(bf16[64,2304]{1,0:T(8,128)(2,1)S(1)} %pad_maximum_fusion.6), channel_id=1, source_target_pairs={{0,1},{1,2},{2,3},{3,0},{4,5},{5,6},{6,7},{7,4},{8,9},{9,10},{10,1... | collective-permute-start | bytes 884744 | tf_op jit(solution)/shard_map/ppermute | solution.py:105
  157.6 12.6 %collective-permute-start.15 = (bf16[64,2304]{1,0:T(8,128)(2,1)S(1)}, bf16[64,2304]{1,0:T(8,128)(2,1)S(1)}, u32[]{:S(2)}, u32[]{:S(2)}) collective-permute-start(bf16[64,2304]{1,0:T(8,128)(2,1)S(1)} %pad_maximum_fusion.7), channel_id=1, source_target_pairs={{0,3},{1,0},{2,1},{3,2},{4,7},{5,4},{6,5},{7,6},{8,11},{9,8},{10,9... | collective-permute-start | bytes 884744 | tf_op jit(solution)/shard_map/ppermute | solution.py:105
  162.8 10.8 %collective-permute-start.21 = (bf16[64,2304]{1,0:T(8,128)(2,1)S(1)}, bf16[64,2304]{1,0:T(8,128)(2,1)S(1)}, u32[]{:S(2)}, u32[]{:S(2)}) collective-permute-start(bf16[64,2304]{1,0:T(8,128)(2,1)S(1)} %pad_maximum_fusion.8), channel_id=1, source_target_pairs={{0,1},{1,2},{2,3},{3,0},{4,5},{5,6},{6,7},{7,4},{8,9},{9,10},{10,1... | collective-permute-start | bytes 884744 | tf_op jit(solution)/shard_map/ppermute | solution.py:105
  165.0 10.1 %collective-permute-start.23 = (bf16[64,2304]{1,0:T(8,128)(2,1)S(1)}, bf16[64,2304]{1,0:T(8,128)(2,1)S(1)}, u32[]{:S(2)}, u32[]{:S(2)}) collective-permute-start(bf16[64,2304]{1,0:T(8,128)(2,1)S(1)} %pad_maximum_fusion.9), channel_id=1, source_target_pairs={{0,3},{1,0},{2,1},{3,2},{4,7},{5,4},{6,5},{7,6},{8,11},{9,8},{10,9... | collective-permute-start | bytes 884744 | tf_op jit(solution)/shard_map/ppermute | solution.py:105
  170.3 7.7 %collective-permute-start.16 = (bf16[2,16,2304]{2,1,0:T(8,128)(2,1)S(1)}, bf16[2,16,2304]{2,1,0:T(8,128)(2,1)S(1)}, u32[]{:S(2)}, u32[]{:S(2)}) collective-permute-start(bf16[2,16,2304]{2,1,0:T(8,128)(2,1)S(1)} %fusion.44), channel_id=1, source_target_pairs={{0,4},{1,5},{2,6},{3,7},{4,0},{5,1},{6,2},{7,3},{8,12},{9,13},{10,... | collective-permute-start | bytes 442376 | tf_op jit(solution)/shard_map/ppermute | solution.py:59
  175.2 10.3 %copy-start.17 = (f32[256,32]{0,1:T(8,128)S(1)}, f32[256,32]{0,1:T(8,128)}, u32[]{:S(2)}) copy-start(f32[256,32]{0,1:T(8,128)} %fusion.63) | copy-start | bytes 98308
  175.2 15.4 %copy-start.8 = (f32[16,2304]{1,0:T(8,128)S(1)}, f32[16,2304]{1,0:T(8,128)}, u32[]{:S(2)}) copy-start(f32[16,2304]{1,0:T(8,128)} %reshape.284) | copy-start | bytes 442372
  175.2 15.4 %copy-start.9 = (f32[16,2304]{1,0:T(8,128)S(1)}, f32[16,2304]{1,0:T(8,128)}, u32[]{:S(2)}) copy-start(f32[16,2304]{1,0:T(8,128)} %reshape.286) | copy-start | bytes 442372
  175.3 7.9 %collective-permute-start.24 = (bf16[2,16,2304]{2,1,0:T(8,128)(2,1)S(1)}, bf16[2,16,2304]{2,1,0:T(8,128)(2,1)S(1)}, u32[]{:S(2)}, u32[]{:S(2)}) collective-permute-start(bf16[2,16,2304]{2,1,0:T(8,128)(2,1)S(1)} %fusion.45), channel_id=1, source_target_pairs={{0,4},{1,5},{2,6},{3,7},{4,0},{5,1},{6,2},{7,3},{8,12},{9,13},{10,... | collective-permute-start | bytes 442376 | tf_op jit(solution)/shard_map/ppermute | solution.py:59
  178.1 9.4 %collective-permute-start.17 = (bf16[16,2304]{1,0:T(8,128)(2,1)S(1)}, bf16[16,2304]{1,0:T(8,128)(2,1)S(1)}, u32[]{:S(2)}, u32[]{:S(2)}) collective-permute-start(bf16[16,2304]{1,0:T(8,128)(2,1)S(1)} %fusion.61), channel_id=1, source_target_pairs={{0,8},{1,9},{2,10},{3,11},{4,12},{5,13},{6,14},{7,15},{8,0},{9,1},... | collective-permute-start | bytes 221192 | tf_op jit(solution)/shard_map/ppermute | solution.py:59
  183.3 7.3 %collective-permute-start.25 = (bf16[16,2304]{1,0:T(8,128)(2,1)S(1)}, bf16[16,2304]{1,0:T(8,128)(2,1)S(1)}, u32[]{:S(2)}, u32[]{:S(2)}) collective-permute-start(bf16[16,2304]{1,0:T(8,128)(2,1)S(1)} %fusion.62), channel_id=1, source_target_pairs={{0,8},{1,9},{2,10},{3,11},{4,12},{5,13},{6,14},{7,15},{8,0},{9,1},... | collective-permute-start | bytes 221192 | tf_op jit(solution)/shard_map/ppermute | solution.py:59
  190.7 7.5 %collective-permute-start.26 = (bf16[16,2304]{1,0:T(8,128)(2,1)S(1)}, bf16[16,2304]{1,0:T(8,128)(2,1)}, u32[]{:S(2)}, u32[]{:S(2)}) collective-permute-start(bf16[16,2304]{1,0:T(8,128)(2,1)S(1)} %get-tuple-element.25), channel_id=1, source_target_pairs={{0,8},{1,9},{2,10},{3,11},{4,12},{5,13},{6,14},{7,15},{8,0},{9,1},... | collective-permute-start | bytes 221192 | tf_op jit(solution)/shard_map/ppermute | solution.py:59
  192.9 8.3 %collective-permute-start.18 = (bf16[16,2304]{1,0:T(8,128)(2,1)S(1)}, bf16[16,2304]{1,0:T(8,128)(2,1)S(1)}, u32[]{:S(2)}, u32[]{:S(2)}) collective-permute-start(bf16[16,2304]{1,0:T(8,128)(2,1)S(1)} %get-tuple-element.26), channel_id=1, source_target_pairs={{0,8},{1,9},{2,10},{3,11},{4,12},{5,13},{6,14},{7,15},{8,0},{9,1},... | collective-permute-start | bytes 221192 | tf_op jit(solution)/shard_map/ppermute | solution.py:59
  199.2 7.0 %collective-permute-start.27 = (bf16[2,16,2304]{2,1,0:T(8,128)(2,1)S(1)}, bf16[2,16,2304]{2,1,0:T(8,128)(2,1)S(1)}, u32[]{:S(2)}, u32[]{:S(2)}) collective-permute-start(bf16[2,16,2304]{2,1,0:T(8,128)(2,1)S(1)} %maximum_select_fusion.4), channel_id=1, source_target_pairs={{0,4},{1,5},{2,6},{3,7},{4,0},{5,1},{6,2},{7,3},{8,12},{9,13},{10,... | collective-permute-start | bytes 442376 | tf_op jit(solution)/shard_map/ppermute | solution.py:59
  201.2 13.4 %collective-permute-start.19 = (bf16[2,16,2304]{2,1,0:T(8,128)(2,1)S(1)}, bf16[2,16,2304]{2,1,0:T(8,128)(2,1)S(1)}, u32[]{:S(2)}, u32[]{:S(2)}) collective-permute-start(bf16[2,16,2304]{2,1,0:T(8,128)(2,1)S(1)} %maximum_select_fusion.3), channel_id=1, source_target_pairs={{0,4},{1,5},{2,6},{3,7},{4,0},{5,1},{6,2},{7,3},{8,12},{9,13},{10,... | collective-permute-start | bytes 442376 | tf_op jit(solution)/shard_map/ppermute | solution.py:59
  207.0 10.6 %collective-permute-start.28 = (bf16[64,2304]{1,0:T(8,128)(2,1)}, bf16[64,2304]{1,0:T(8,128)(2,1)}, u32[]{:S(2)}, u32[]{:S(2)}) collective-permute-start(bf16[64,2304]{1,0:T(8,128)(2,1)} %bitcast.72), channel_id=1, source_target_pairs={{0,1},{1,2},{2,3},{3,0},{4,5},{5,6},{6,7},{7,4},{8,9},{9,10},{10,1... | collective-permute-start | bytes 884744 | tf_op jit(solution)/shard_map/ppermute | solution.py:105
  209.0 11.5 %collective-permute-start.29 = (bf16[64,2304]{1,0:T(8,128)(2,1)}, bf16[64,2304]{1,0:T(8,128)(2,1)}, u32[]{:S(2)}, u32[]{:S(2)}) collective-permute-start(bf16[64,2304]{1,0:T(8,128)(2,1)} %bitcast.72), channel_id=1, source_target_pairs={{0,3},{1,0},{2,1},{3,2},{4,7},{5,4},{6,5},{7,6},{8,11},{9,8},{10,9... | collective-permute-start | bytes 884744 | tf_op jit(solution)/shard_map/ppermute | solution.py:105
  218.6 10.0 %collective-permute-start.30 = (bf16[64,1152]{1,0:T(8,128)(2,1)S(1)}, bf16[64,1152]{1,0:T(8,128)(2,1)S(1)}, u32[]{:S(2)}, u32[]{:S(2)}) collective-permute-start(bf16[64,1152]{1,0:T(8,128)(2,1)S(1)} %slice.199), channel_id=1, source_target_pairs={{0,1},{1,2},{2,3},{3,0},{4,5},{5,6},{6,7},{7,4},{8,9},{9,10},{10,1... | collective-permute-start | bytes 442376 | tf_op jit(solution)/shard_map/ppermute | solution.py:105
  221.4 9.7 %collective-permute-start.31 = (bf16[64,1152]{1,0:T(8,128)(2,1)S(1)}, bf16[64,1152]{1,0:T(8,128)(2,1)S(1)}, u32[]{:S(2)}, u32[]{:S(2)}) collective-permute-start(bf16[64,1152]{1,0:T(8,128)(2,1)S(1)} %slice.200), channel_id=1, source_target_pairs={{0,3},{1,0},{2,1},{3,2},{4,7},{5,4},{6,5},{7,6},{8,11},{9,8},{10,9... | collective-permute-start | bytes 442376 | tf_op jit(solution)/shard_map/ppermute | solution.py:105
  231.1 1.0 copy-start.4
  242.3 1.7 copy-start.6
  243.9 1.1 copy-start.20
  245.0 2.6 copy-start.5
  248.2 1.3 copy-start.1
  250.6 5.5 %collective-permute-start.33 = (bf16[8,72,864]{2,1,0:T(8,128)(2,1)S(1)}, bf16[8,72,864]{2,1,0:T(8,128)(2,1)S(1)}, u32[]{:S(2)}, u32[]{:S(2)}) collective-permute-start(bf16[8,72,864]{2,1,0:T(8,128)(2,1)S(1)} %bitcast.205), channel_id=1, source_target_pairs={{0,16},{16,0},{32,48},{48,32},{64,80},{80,64},{96,112},{112,96},{1... | collective-permute-start | bytes 2985992 | tf_op jit(solution)/shard_map/ppermute | solution.py:55
  253.7 4.7 %collective-permute-start.32 = (bf16[8,72,864]{2,1,0:T(8,128)(2,1)S(1)}, bf16[8,72,864]{2,1,0:T(8,128)(2,1)S(1)}, u32[]{:S(2)}, u32[]{:S(2)}) collective-permute-start(bf16[8,72,864]{2,1,0:T(8,128)(2,1)S(1)} %bitcast.206), channel_id=1, source_target_pairs={{0,16},{16,0},{32,48},{48,32},{64,80},{80,64},{96,112},{112,96},{1... | collective-permute-start | bytes 2985992 | tf_op jit(solution)/shard_map/ppermute | solution.py:55
  260.0 44.5 %all-to-all-start.1 = ((bf16[8,72,1152]{2,1,0:T(8,128)(2,1)}), bf16[8,72,1152]{2,1,0:T(8,128)(2,1)S(1)}, u32[]{:S(2)}, u32[]{:S(2)}) async-start(bf16[8,72,1152]{2,1,0:T(8,128)(2,1)} %pad_maximum_fusion.2), calls=%async_computation.1 | async-start | bytes 2654208 | tf_op jit(solution)/shard_map/all_to_all | solution.py:76
  267.4 50.6 %reduce-scatter.4.cloned.1.call-start = ((), (), s32[]{:S(2)}) async-start(), calls=%async_computation.5 | async-start | bytes 829440
  268.7 50.4 %copy-start.14 = (f32[288,72]{0,1:T(8,128)S(1)}, f32[288,72]{0,1:T(8,128)}, u32[]{:S(2)}) copy-start(f32[288,72]{0,1:T(8,128)} %param.25) | copy-start | bytes 248836
  268.7 51.1 %copy-start.11 = (bf16[72,288]{1,0:T(8,128)(2,1)S(1)}, bf16[72,288]{1,0:T(8,128)(2,1)}, u32[]{:S(2)}) copy-start(bf16[72,288]{1,0:T(8,128)(2,1)} %param.20) | copy-start | bytes 124420
  268.7 51.1 %copy-start.12 = (bf16[72,288]{1,0:T(8,128)(2,1)S(1)}, bf16[72,288]{1,0:T(8,128)(2,1)}, u32[]{:S(2)}) copy-start(bf16[72,288]{1,0:T(8,128)(2,1)} %param.21) | copy-start | bytes 124420
  268.8 51.1 %copy-start.15 = (f32[72,288]{1,0:T(8,128)S(1)}, f32[72,288]{1,0:T(8,128)}, u32[]{:S(2)}) copy-start(f32[72,288]{1,0:T(8,128)} %param.24) | copy-start | bytes 248836
  268.8 51.1 %copy-start.16 = (f32[72,288]{1,0:T(8,128)S(1)}, f32[72,288]{1,0:T(8,128)}, u32[]{:S(2)}) copy-start(f32[72,288]{1,0:T(8,128)} %param.23) | copy-start | bytes 248836
  304.7 14.2 %collective-permute-start.34 = (bf16[72,864]{1,0:T(8,128)(2,1)S(1)}, bf16[72,864]{1,0:T(8,128)(2,1)S(1)}, u32[]{:S(2)}, u32[]{:S(2)}) collective-permute-start(bf16[72,864]{1,0:T(8,128)(2,1)S(1)} %slice.308), channel_id=1, source_target_pairs={{0,256},{16,272},{32,288},{48,304},{64,320},{80,336},{96,352},{112... | collective-permute-start | bytes 373256 | tf_op jit(solution)/shard_map/ppermute | solution.py:55
Sparse Core Ops, SparseCore 0:
  37.1 45.3 all-gather.5
  215.5 26.7 all-gather.3
  271.1 46.8 reduce-scatter.3

commit v2 on v0

--- a/solution.py
+++ b/solution.py
@@ -44,13 +44,6 @@
     return beta_decay * ema + (1.0 - beta_decay) * (probe.astype(F32) * hvp)
 
 
-def ring_step(array):
-    perm = [
-        (s, (s // 16) * 16 + ((s // 2 % 8 + (1 - 2 * (s % 2))) % 8) * 2 + s % 2) for s in range(32)
-    ]
-    return lax.ppermute(array, "seq", perm)
-
-
 def seq_swap(array, bit):
     return lax.ppermute(array, "seq", [(s, s ^ bit) for s in range(32)])
 
@@ -76,24 +69,29 @@
     return lax.all_to_all(array, axis, 0, 0, axis_index_groups=groups)
 
 
-def after(array, *earlier):
-    for other in earlier:
-        array = array + 0 * other[(slice(0, 1),) * other.ndim].reshape((1,) * array.ndim)
-    return array
-
-
-def ring_chunks(chunk):
-    held = [chunk]
-    for k in range(1, NZ):
-        held.append(ring_step(held[-1]))
-    return held
-
-
-def in_order(held, z, sign):
-    own = jnp.zeros((NZ,) + held[0].shape, held[0].dtype)
-    for k, chunk in enumerate(held):
-        own = lax.dynamic_update_slice(own, chunk[None], ((z - sign * k) % NZ, 0, 0))
-    return own
+def z_shift(array, by):
+    perm = [(s, (s // 16) * 16 + ((s // 2 % 8 + by) % 8) * 2 + s % 2) for s in range(32)]
+    return lax.ppermute(array, "seq", perm)
+
+
+def gather_z(chunk, z):
+    r, rows, n = chunk.shape
+    h = 128 * ((n + 255) // 256) if n > 128 else n // 2
+    buf = jnp.zeros((r, NZ, rows, n), chunk.dtype)
+
+    def put(buf, piece, at, col=0):
+        return lax.dynamic_update_slice(buf, piece[:, None], (0, (z + at) % NZ, 0, col))
+
+    buf = put(buf, chunk, 0)
+    up = down = chunk
+    for k in (1, 2, 3):
+        up = z_shift(up, 1)
+        down = z_shift(down, -1)
+        buf = put(buf, up, NZ - k)
+        buf = put(buf, down, k)
+    buf = put(buf, z_shift(up[:, :, :h], 1), 4)
+    buf = put(buf, z_shift(down[:, :, h:], -1), 4, h)
+    return buf
 
 
 def exchange_sum(parts, axis, groups):
@@ -209,7 +207,6 @@
     yh, z, c = s // 16, (s // 2) % 8, s % 2
     yl, x = t // 4, t % 4
 
-    sign = 1 - 2 * c
     labels = jnp.arange(32, dtype=jnp.int32)
     onehot = (segment_ids[:, None] == labels[None, :]).astype(F32)
 
@@ -217,25 +214,20 @@
     tally = jnp.pad(jnp.sum(onehot, axis=0).astype(BF)[None], ((0, ROWS - 1), (0, TALLY - 32)))
     own_out = jnp.concatenate([w_down.T, dir_down.T, tally], axis=1)
     across_in = seq_swap(own_in, 16)
-    near_held = ring_chunks(own_in)
-    near = in_order(near_held, z, sign)
-    own_out = after(own_out, near_held[1])
     outs = group_gather(jnp.stack([own_out, seq_swap(own_out, 16)]), "seq", Z_GROUPS)
-    near_other = seq_swap(near, 1)
-    away = in_order(ring_chunks(across_in), z, sign)
+    ins = gather_z(jnp.stack([own_in, across_in]), z)
     outs_other = seq_swap(outs, 1)
-    away_other = seq_swap(away, 1)
-
-    tokens = after(tokens, near_held[-1])
-    target = after(target, near_held[-1])
+    ins_other = seq_swap(ins, 1)
+
     wide = tokens.astype(F32)
     scale = lax.rsqrt(jnp.mean(wide * wide, axis=1, keepdims=True) + norm_eps)
     normed = (wide * scale * norm_gain).astype(BF)
     normed = relative(normed, yh, c)
 
     half = 2 * NZ * ROWS
-    near_all = jnp.stack([near, near_other]).reshape(half, 4 * UNITS)
-    away_all = jnp.stack([away, away_other]).reshape(half, 4 * UNITS)
+    near_all, away_all = (
+        jnp.stack([ins[i], ins_other[i]]).reshape(half, 4 * UNITS) for i in range(2)
+    )
     pre = product(normed[:, :half], near_all) + product(normed[:, half:], away_all)
     gate, upper, gate_dot, upper_dot = (pre[:, i * UNITS : (i + 1) * UNITS] for i in range(4))
     value, first, second = gelu_parts(gate)

time: 312 us -> 294 us (0.942)
  starting transfers between devices: 163 us -> 146 us
    ppermute x14 -> x8, starting transfers between devices: 48.4 us -> 34.6 us  [z_shift(): return lax.ppermute(array, 'seq', perm)]
    dynamic_update_slice x16 -> x8, local copies, waits for them, and re-layouts: 10.3 us -> 6.02 us  [put(): lax.dynamic_update_slice(buf, piece[:, None], (0, (z + at) % NZ, 0, col))]
    slice x2 -> x4, local copies, waits for them, and re-layouts: 1.7 us -> 5.48 us  [the longest x1 3.52 us: per_device(): ins[i]]
    ppermute x14 -> x8, waiting for transfers between devices: 14.9 us -> 13.9 us  [z_shift(): return lax.ppermute(array, 'seq', perm)]
    ppermute x8 -> x7, starting transfers between devices: 25.1 us -> 24.3 us  [seq_swap(): return lax.ppermute(array, 'seq', [(s, s ^ bit) for s in range(32)])]
  transfers between devices with their start and end apart: 49 -> 42, of which waited for: 21 -> 19; matrix products, arithmetic and copies ran while one was open for 13% -> 15% of each run, Pallas kernels for 0% -> 0%
where the time goes in v2:
time: 294 us; the launch traced here: 291 us
  starting transfers between devices  146 us (50%)
  waiting for transfers between devices  70.6 us (24%)
  local copies, waits for them, and re-layouts  27.7 us (9%)
  other arithmetic  19.7 us (7%)
  between operations  15.5 us (5%)
  matrix products  11 us (4%)
    ppermute x16, starting transfers between devices, x_shift(): return lax.ppermute(array, 'tensor', perm)  56.6 us
    all_to_all x1, waiting for transfers between devices, group_exchange(): return lax.all_to_all(array, axis, 0, 0, axis_index_groups=groups)  34.7 us
    ppermute x8, starting transfers between devices, z_shift(): return lax.ppermute(array, 'seq', perm)  34.6 us
    ppermute x8, starting transfers between devices, y_swap(): return lax.ppermute(array, 'tensor', [(t, t ^ bit * 4) for t in range(16)])  25.6 us
    ppermute x7, starting transfers between devices, seq_swap(): return lax.ppermute(array, 'seq', [(s, s ^ bit) for s in range(32)])  24.3 us
    ppermute x8, waiting for transfers between devices, z_shift(): return lax.ppermute(array, 'seq', perm)  13.9 us
    unnamed x3, waiting for transfers between devices  8.66 us
    ppermute x8, waiting for transfers between devices, y_swap(): return lax.ppermute(array, 'tensor', [(t, t ^ bit * 4) for t in range(16)])  7.21 us
  transfers between devices with their start and end apart: 42, of which 19 were waited for; matrix products, arithmetic and copies ran while one was open for 15% of the time, Pallas kernels for 0%

profile of v2, /device:TPU:56, one launch (start us, length us, event | category | flops | bytes accessed | tf_op | source)
XLA Modules:
  0.0 290.6 jit_solution(3827900401115948777)
XLA Ops:
  7.2 1.8 concatenate.64
  9.0 4.7 %collective-permute-start = (bf16[72,1152]{1,0:T(8,128)(2,1)}, bf16[72,1152]{1,0:T(8,128)(2,1)}, u32[]{:S(2)}, u32[]{:S(2)}) collective-permute-start(bf16[72,1152]{1,0:T(8,128)(2,1)} %concatenate.64), channel_id=1, source_target_pairs={{0,256},{16,272},{32,288},{48,304},{64,320},{80,336},{96,352},{112... | collective-permute-start | bytes 497672 | tf_op jit(solution)/shard_map/ppermute | solution.py:48
  14.5 1.6 fusion.60
  16.1 5.2 %collective-permute-start.10 = (bf16[72,640]{1,0:T(8,128)(2,1)}, bf16[72,640]{1,0:T(8,128)(2,1)}, u32[]{:S(2)}, u32[]{:S(2)}) collective-permute-start(bf16[72,640]{1,0:T(8,128)(2,1)} %fusion.60), channel_id=1, source_target_pairs={{0,256},{16,272},{32,288},{48,304},{64,320},{80,336},{96,352},{112... | collective-permute-start | bytes 276488 | tf_op jit(solution)/shard_map/ppermute | solution.py:48
  21.3 1.6 copy.141
  24.9 1.8 pad_maximum_fusion.5
  26.7 4.3 %collective-permute-start.1 = (bf16[2,72,1152]{2,1,0:T(8,128)(2,1)}, bf16[2,72,1152]{2,1,0:T(8,128)(2,1)S(1)}, u32[]{:S(2)}, u32[]{:S(2)}) collective-permute-start(bf16[2,72,1152]{2,1,0:T(8,128)(2,1)} %pad_maximum_fusion.5), channel_id=1, source_target_pairs={{0,32},{16,48},{32,64},{48,80},{64,96},{80,112},{96,128},{112,144}... | collective-permute-start | bytes 995336 | tf_op jit(solution)/shard_map/ppermute | solution.py:74
  31.0 8.6 %collective-permute-start.2 = (bf16[2,72,1152]{2,1,0:T(8,128)(2,1)}, bf16[2,72,1152]{2,1,0:T(8,128)(2,1)S(1)}, u32[]{:S(2)}, u32[]{:S(2)}) collective-permute-start(bf16[2,72,1152]{2,1,0:T(8,128)(2,1)} %pad_maximum_fusion.5), channel_id=1, source_target_pairs={{0,224},{16,240},{32,0},{48,16},{64,32},{80,48},{96,64},{112,80},{... | collective-permute-start | bytes 995336 | tf_op jit(solution)/shard_map/ppermute | solution.py:74
  39.6 1.6 pad_maximum_fusion.11
  41.2 1.7 broadcast_in_dim.61
  42.9 1.8 bitcast_dynamic-update-slice_fusion.6
  45.3 1.9 collective-permute-start.3
  47.3 5.1 %collective-permute-start.4 = (bf16[2,72,1152]{2,1,0:T(8,128)(2,1)S(1)}, bf16[2,72,1152]{2,1,0:T(8,128)(2,1)S(1)}, u32[]{:S(2)}, u32[]{:S(2)}) collective-permute-start(bf16[2,72,1152]{2,1,0:T(8,128)(2,1)S(1)} %collective-permute-done.2), channel_id=1, source_target_pairs={{0,224},{16,240},{32,0},{48,16},{64,32},{80,48},{96,64},{112,80},{... | collective-permute-start | bytes 995336 | tf_op jit(solution)/shard_map/ppermute | solution.py:74
  53.9 3.2 %collective-permute-done.3 = bf16[2,72,1152]{2,1,0:T(8,128)(2,1)S(1)} collective-permute-done((bf16[2,72,1152]{2,1,0:T(8,128)(2,1)S(1)}, bf16[2,72,1152]{2,1,0:T(8,128)(2,1)S(1)}, u32[]{:S(2)}, u32[]{:S(2)}) %collective-permute-start.3) | collective-permute-done | bytes 331808 | tf_op jit(solution)/shard_map/ppermute | solution.py:74
  57.1 1.9 collective-permute-start.5
  59.0 1.2 collective-permute-done.4
  60.2 5.6 %collective-permute-start.6 = (bf16[2,72,1152]{2,1,0:T(8,128)(2,1)S(1)}, bf16[2,72,1152]{2,1,0:T(8,128)(2,1)S(1)}, u32[]{:S(2)}, u32[]{:S(2)}) collective-permute-start(bf16[2,72,1152]{2,1,0:T(8,128)(2,1)S(1)} %collective-permute-done.4), channel_id=1, source_target_pairs={{0,224},{16,240},{32,0},{48,16},{64,32},{80,48},{96,64},{112,80},{... | collective-permute-start | bytes 995336 | tf_op jit(solution)/shard_map/ppermute | solution.py:74
  67.4 7.7 %collective-permute-done.5 = bf16[2,72,1152]{2,1,0:T(8,128)(2,1)S(1)} collective-permute-done((bf16[2,72,1152]{2,1,0:T(8,128)(2,1)S(1)}, bf16[2,72,1152]{2,1,0:T(8,128)(2,1)S(1)}, u32[]{:S(2)}, u32[]{:S(2)}) %collective-permute-start.5) | collective-permute-done | bytes 331808 | tf_op jit(solution)/shard_map/ppermute | solution.py:74
  75.1 1.9 collective-permute-start.7
  77.1 5.3 %collective-permute-start.8 = (bf16[2,72,512]{2,1,0:T(8,128)(2,1)S(1)}, bf16[2,72,512]{2,1,0:T(8,128)(2,1)S(1)}, u32[]{:S(2)}, u32[]{:S(2)}) collective-permute-start(bf16[2,72,512]{2,1,0:T(8,128)(2,1)S(1)} %slice.203), channel_id=1, source_target_pairs={{0,224},{16,240},{32,0},{48,16},{64,32},{80,48},{96,64},{112,80},{... | collective-permute-start | bytes 442376 | tf_op jit(solution)/shard_map/ppermute | solution.py:74
  86.5 1.9 collective-permute-start.9
  88.4 1.5 constant_dynamic-slice_fusion.1
  94.2 3.5 %fusion.69 = (bf16[1,8,72,1152]{3,2,1,0:T(8,128)(2,1)S(1)}, bf16[1,8,72,1152]{3,2,1,0:T(8,128)(2,1)}) fusion(bf16[2,8,72,1152]{3,2,1,0:T(8,128)(2,1)} %bitcast_dynamic-update-slice_fusion.16), kind=kLoop, calls=%fused_computation.173 | loop fusion | bytes 5308416 | tf_op jit(solution)/shard_map/slice | solution.py:229
  97.8 1.5 copy.151
  99.3 2.5 collective-permute-start.11
  101.8 1.9 fusion.70
  110.8 3.1 %collective-permute-start.12 = (bf16[64,1152]{1,0:T(8,128)(2,1)S(1)}, bf16[64,1152]{1,0:T(8,128)(2,1)S(1)}, u32[]{:S(2)}, u32[]{:S(2)}) collective-permute-start(bf16[64,1152]{1,0:T(8,128)(2,1)S(1)} %get-tuple-element.23), channel_id=1, source_target_pairs={{0,1},{1,2},{2,3},{3,0},{4,5},{5,6},{6,7},{7,4},{8,9},{9,10},{10,1... | collective-permute-start | bytes 442376 | tf_op jit(solution)/shard_map/ppermute | solution.py:103
  113.9 3.9 %collective-permute-start.14 = (bf16[64,1152]{1,0:T(8,128)(2,1)S(1)}, bf16[64,1152]{1,0:T(8,128)(2,1)S(1)}, u32[]{:S(2)}, u32[]{:S(2)}) collective-permute-start(bf16[64,1152]{1,0:T(8,128)(2,1)S(1)} %get-tuple-element.24), channel_id=1, source_target_pairs={{0,3},{1,0},{2,1},{3,2},{4,7},{5,4},{6,5},{7,6},{8,11},{9,8},{10,9... | collective-permute-start | bytes 442376 | tf_op jit(solution)/shard_map/ppermute | solution.py:103
  118.0 1.9 collective-permute-start.24
  119.9 5.1 %collective-permute-start.26 = (bf16[64,1152]{1,0:T(8,128)(2,1)S(1)}, bf16[64,1152]{1,0:T(8,128)(2,1)S(1)}, u32[]{:S(2)}, u32[]{:S(2)}) collective-permute-start(bf16[64,1152]{1,0:T(8,128)(2,1)S(1)} %get-tuple-element.22), channel_id=1, source_target_pairs={{0,3},{1,0},{2,1},{3,2},{4,7},{5,4},{6,5},{7,6},{8,11},{9,8},{10,9... | collective-permute-start | bytes 442376 | tf_op jit(solution)/shard_map/ppermute | solution.py:103
  125.3 1.9 collective-permute-start.13
  127.3 5.1 %collective-permute-start.15 = (bf16[64,2304]{1,0:T(8,128)(2,1)S(1)}, bf16[64,2304]{1,0:T(8,128)(2,1)S(1)}, u32[]{:S(2)}, u32[]{:S(2)}) collective-permute-start(bf16[64,2304]{1,0:T(8,128)(2,1)S(1)} %pad_maximum_fusion.8), channel_id=1, source_target_pairs={{0,3},{1,0},{2,1},{3,2},{4,7},{5,4},{6,5},{7,6},{8,11},{9,8},{10,9... | collective-permute-start | bytes 884744 | tf_op jit(solution)/shard_map/ppermute | solution.py:103
  132.5 1.9 collective-permute-start.25
  134.6 5.3 %collective-permute-start.27 = (bf16[64,2304]{1,0:T(8,128)(2,1)S(1)}, bf16[64,2304]{1,0:T(8,128)(2,1)S(1)}, u32[]{:S(2)}, u32[]{:S(2)}) collective-permute-start(bf16[64,2304]{1,0:T(8,128)(2,1)S(1)} %pad_maximum_fusion.10), channel_id=1, source_target_pairs={{0,3},{1,0},{2,1},{3,2},{4,7},{5,4},{6,5},{7,6},{8,11},{9,8},{10,9... | collective-permute-start | bytes 884744 | tf_op jit(solution)/shard_map/ppermute | solution.py:103
  140.1 2.7 collective-permute-start.16
  142.9 1.3 collective-permute-done.27
  144.3 2.5 collective-permute-start.28
  146.9 1.9 collective-permute-done.16
  148.8 4.9 %collective-permute-start.17 = (bf16[16,2304]{1,0:T(8,128)(2,1)S(1)}, bf16[16,2304]{1,0:T(8,128)(2,1)S(1)}, u32[]{:S(2)}, u32[]{:S(2)}) collective-permute-start(bf16[16,2304]{1,0:T(8,128)(2,1)S(1)} %fusion.61), channel_id=1, source_target_pairs={{0,8},{1,9},{2,10},{3,11},{4,12},{5,13},{6,14},{7,15},{8,0},{9,1},... | collective-permute-start | bytes 221192 | tf_op jit(solution)/shard_map/ppermute | solution.py:52
  153.8 3.3 %collective-permute-start.29 = (bf16[16,2304]{1,0:T(8,128)(2,1)S(1)}, bf16[16,2304]{1,0:T(8,128)(2,1)S(1)}, u32[]{:S(2)}, u32[]{:S(2)}) collective-permute-start(bf16[16,2304]{1,0:T(8,128)(2,1)S(1)} %fusion.62), channel_id=1, source_target_pairs={{0,8},{1,9},{2,10},{3,11},{4,12},{5,13},{6,14},{7,15},{8,0},{9,1},... | collective-permute-start | bytes 221192 | tf_op jit(solution)/shard_map/ppermute | solution.py:52
  158.2 3.3 %collective-permute-done.29 = bf16[16,2304]{1,0:T(8,128)(2,1)S(1)} collective-permute-done((bf16[16,2304]{1,0:T(8,128)(2,1)S(1)}, bf16[16,2304]{1,0:T(8,128)(2,1)S(1)}, u32[]{:S(2)}, u32[]{:S(2)}) %collective-permute-start.29) | collective-permute-done | bytes 73760 | tf_op jit(solution)/shard_map/ppermute | solution.py:52
  161.6 2.8 collective-permute-start.30
  164.3 4.0 %collective-permute-start.18 = (bf16[16,2304]{1,0:T(8,128)(2,1)S(1)}, bf16[16,2304]{1,0:T(8,128)(2,1)S(1)}, u32[]{:S(2)}, u32[]{:S(2)}) collective-permute-start(bf16[16,2304]{1,0:T(8,128)(2,1)S(1)} %get-tuple-element.28), channel_id=1, source_target_pairs={{0,8},{1,9},{2,10},{3,11},{4,12},{5,13},{6,14},{7,15},{8,0},{9,1},... | collective-permute-start | bytes 221192 | tf_op jit(solution)/shard_map/ppermute | solution.py:52
  169.8 1.9 collective-permute-start.31
  172.2 3.5 %collective-permute-start.19 = (bf16[2,16,2304]{2,1,0:T(8,128)(2,1)S(1)}, bf16[2,16,2304]{2,1,0:T(8,128)(2,1)S(1)}, u32[]{:S(2)}, u32[]{:S(2)}) collective-permute-start(bf16[2,16,2304]{2,1,0:T(8,128)(2,1)S(1)} %maximum_select_fusion.3), channel_id=1, source_target_pairs={{0,4},{1,5},{2,6},{3,7},{4,0},{5,1},{6,2},{7,3},{8,12},{9,13},{10,... | collective-permute-start | bytes 442376 | tf_op jit(solution)/shard_map/ppermute | solution.py:52
  176.9 1.9 collective-permute-start.32
  178.9 5.1 %collective-permute-start.33 = (bf16[64,2304]{1,0:T(8,128)(2,1)S(1)}, bf16[64,2304]{1,0:T(8,128)(2,1)S(1)}, u32[]{:S(2)}, u32[]{:S(2)}) collective-permute-start(bf16[64,2304]{1,0:T(8,128)(2,1)S(1)} %bitcast.225), channel_id=1, source_target_pairs={{0,3},{1,0},{2,1},{3,2},{4,7},{5,4},{6,5},{7,6},{8,11},{9,8},{10,9... | collective-permute-start | bytes 884744 | tf_op jit(solution)/shard_map/ppermute | solution.py:103
  184.1 1.9 collective-permute-start.20
  186.0 5.1 %collective-permute-start.21 = (bf16[64,2304]{1,0:T(8,128)(2,1)S(1)}, bf16[64,2304]{1,0:T(8,128)(2,1)S(1)}, u32[]{:S(2)}, u32[]{:S(2)}) collective-permute-start(bf16[64,2304]{1,0:T(8,128)(2,1)S(1)} %bitcast.228), channel_id=1, source_target_pairs={{0,3},{1,0},{2,1},{3,2},{4,7},{5,4},{6,5},{7,6},{8,11},{9,8},{10,9... | collective-permute-start | bytes 884744 | tf_op jit(solution)/shard_map/ppermute | solution.py:103
  191.4 1.9 collective-permute-start.34
  193.4 5.1 %collective-permute-start.35 = (bf16[64,1152]{1,0:T(8,128)(2,1)S(1)}, bf16[64,1152]{1,0:T(8,128)(2,1)S(1)}, u32[]{:S(2)}, u32[]{:S(2)}) collective-permute-start(bf16[64,1152]{1,0:T(8,128)(2,1)S(1)} %slice.230), channel_id=1, source_target_pairs={{0,3},{1,0},{2,1},{3,2},{4,7},{5,4},{6,5},{7,6},{8,11},{9,8},{10,9... | collective-permute-start | bytes 442376 | tf_op jit(solution)/shard_map/ppermute | solution.py:103
  198.6 1.9 collective-permute-start.22
  200.5 5.1 %collective-permute-start.23 = (bf16[64,1152]{1,0:T(8,128)(2,1)S(1)}, bf16[64,1152]{1,0:T(8,128)(2,1)S(1)}, u32[]{:S(2)}, u32[]{:S(2)}) collective-permute-start(bf16[64,1152]{1,0:T(8,128)(2,1)S(1)} %slice.221), channel_id=1, source_target_pairs={{0,3},{1,0},{2,1},{3,2},{4,7},{5,4},{6,5},{7,6},{8,11},{9,8},{10,9... | collective-permute-start | bytes 442376 | tf_op jit(solution)/shard_map/ppermute | solution.py:103
  206.8 1.5 collective-permute-done.23
  210.5 2.6 fusion.39
  216.1 1.9 collective-permute-start.37
  219.2 2.4 collective-permute-start.36
  221.9 1.9 collective-permute-done.36
  224.1 1.4 pad_maximum_fusion.2
  225.5 5.0 %all-to-all-start = ((bf16[8,72,1152]{2,1,0:T(8,128)(2,1)}), bf16[8,72,1152]{2,1,0:T(8,128)(2,1)S(1)}, u32[]{:S(2)}, u32[]{:S(2)}) async-start(bf16[8,72,1152]{2,1,0:T(8,128)(2,1)} %pad_maximum_fusion.2), calls=%async_computation | async-start | bytes 2654208 | tf_op jit(solution)/shard_map/all_to_all | solution.py:69
  230.5 1.3 slice.243
  231.9 34.7 %all-to-all-done = bf16[8,72,1152]{2,1,0:T(8,128)(2,1)S(1)} async-done(((bf16[8,72,1152]{2,1,0:T(8,128)(2,1)}), bf16[8,72,1152]{2,1,0:T(8,128)(2,1)S(1)}, u32[]{:S(2)}, u32[]{:S(2)}) %all-to-all-start) | async-done | bytes 1327136 | tf_op jit(solution)/shard_map/all_to_all | solution.py:69
  266.8 5.6 %collective-permute-start.38 = (bf16[72,864]{1,0:T(8,128)(2,1)S(1)}, bf16[72,864]{1,0:T(8,128)(2,1)S(1)}, u32[]{:S(2)}, u32[]{:S(2)}) collective-permute-start(bf16[72,864]{1,0:T(8,128)(2,1)S(1)} %slice.338), channel_id=1, source_target_pairs={{0,256},{16,272},{32,288},{48,304},{64,320},{80,336},{96,352},{112... | collective-permute-start | bytes 373256 | tf_op jit(solution)/shard_map/ppermute | solution.py:48
  272.5 8.6 %reduce-scatter.4.cloned.1.call-done = bf16[1,72,576]{2,1,0:T(8,128)(2,1)} async-done(((bf16[8,72,576]{2,1,0:T(8,128)(2,1)}), bf16[1,72,576]{2,1,0:T(8,128)(2,1)}) %reduce-scatter.4.cloned.1.call-update) | async-done | bytes 82960
  (180 shorter events, 38.2 us)
Async XLA Ops:
  7.2 84.2 %copy-start = (bf16[256,2304]{1,0:T(8,128)(2,1)S(1)}, bf16[256,2304]{1,0:T(8,128)(2,1)}, u32[]{:S(2)}) copy-start(bf16[256,2304]{1,0:T(8,128)(2,1)} %param.14) | copy-start | bytes 3538948
  7.2 90.6 %all-gather.3.cloned.1.call-start = ((), (), s32[]{:S(2)}) async-start(), calls=%async_computation.2 | async-start | bytes 1658880 | tf_op jit(solution)/shard_map/all_gather | solution.py:61
  9.0 15.9 %collective-permute-start = (bf16[72,1152]{1,0:T(8,128)(2,1)}, bf16[72,1152]{1,0:T(8,128)(2,1)}, u32[]{:S(2)}, u32[]{:S(2)}) collective-permute-start(bf16[72,1152]{1,0:T(8,128)(2,1)} %concatenate.64), channel_id=1, source_target_pairs={{0,256},{16,272},{32,288},{48,304},{64,320},{80,336},{96,352},{112... | collective-permute-start | bytes 497672 | tf_op jit(solution)/shard_map/ppermute | solution.py:48
  16.1 7.1 %copy-start.15 = (f32[2304]{0:T(1024)S(1)}, f32[2304]{0:T(1024)}, u32[]{:S(2)}) copy-start(f32[2304]{0:T(1024)} %param.16) | copy-start | bytes 27652
  16.1 23.5 %collective-permute-start.10 = (bf16[72,640]{1,0:T(8,128)(2,1)}, bf16[72,640]{1,0:T(8,128)(2,1)}, u32[]{:S(2)}, u32[]{:S(2)}) collective-permute-start(bf16[72,640]{1,0:T(8,128)(2,1)} %fusion.60), channel_id=1, source_target_pairs={{0,256},{16,272},{32,288},{48,304},{64,320},{80,336},{96,352},{112... | collective-permute-start | bytes 276488 | tf_op jit(solution)/shard_map/ppermute | solution.py:48
  26.7 18.6 %collective-permute-start.1 = (bf16[2,72,1152]{2,1,0:T(8,128)(2,1)}, bf16[2,72,1152]{2,1,0:T(8,128)(2,1)S(1)}, u32[]{:S(2)}, u32[]{:S(2)}) collective-permute-start(bf16[2,72,1152]{2,1,0:T(8,128)(2,1)} %pad_maximum_fusion.5), channel_id=1, source_target_pairs={{0,32},{16,48},{32,64},{48,80},{64,96},{80,112},{96,128},{112,144}... | collective-permute-start | bytes 995336 | tf_op jit(solution)/shard_map/ppermute | solution.py:74
  31.0 16.3 %collective-permute-start.2 = (bf16[2,72,1152]{2,1,0:T(8,128)(2,1)}, bf16[2,72,1152]{2,1,0:T(8,128)(2,1)S(1)}, u32[]{:S(2)}, u32[]{:S(2)}) collective-permute-start(bf16[2,72,1152]{2,1,0:T(8,128)(2,1)} %pad_maximum_fusion.5), channel_id=1, source_target_pairs={{0,224},{16,240},{32,0},{48,16},{64,32},{80,48},{96,64},{112,80},{... | collective-permute-start | bytes 995336 | tf_op jit(solution)/shard_map/ppermute | solution.py:74
  45.3 11.7 %collective-permute-start.3 = (bf16[2,72,1152]{2,1,0:T(8,128)(2,1)S(1)}, bf16[2,72,1152]{2,1,0:T(8,128)(2,1)S(1)}, u32[]{:S(2)}, u32[]{:S(2)}) collective-permute-start(bf16[2,72,1152]{2,1,0:T(8,128)(2,1)S(1)} %collective-permute-done.1), channel_id=1, source_target_pairs={{0,32},{16,48},{32,64},{48,80},{64,96},{80,112},{96,128},{112,144}... | collective-permute-start | bytes 995336 | tf_op jit(solution)/shard_map/ppermute | solution.py:74
  47.3 13.0 %collective-permute-start.4 = (bf16[2,72,1152]{2,1,0:T(8,128)(2,1)S(1)}, bf16[2,72,1152]{2,1,0:T(8,128)(2,1)S(1)}, u32[]{:S(2)}, u32[]{:S(2)}) collective-permute-start(bf16[2,72,1152]{2,1,0:T(8,128)(2,1)S(1)} %collective-permute-done.2), channel_id=1, source_target_pairs={{0,224},{16,240},{32,0},{48,16},{64,32},{80,48},{96,64},{112,80},{... | collective-permute-start | bytes 995336 | tf_op jit(solution)/shard_map/ppermute | solution.py:74
  57.1 18.0 %collective-permute-start.5 = (bf16[2,72,1152]{2,1,0:T(8,128)(2,1)S(1)}, bf16[2,72,1152]{2,1,0:T(8,128)(2,1)S(1)}, u32[]{:S(2)}, u32[]{:S(2)}) collective-permute-start(bf16[2,72,1152]{2,1,0:T(8,128)(2,1)S(1)} %collective-permute-done.3), channel_id=1, source_target_pairs={{0,32},{16,48},{32,64},{48,80},{64,96},{80,112},{96,128},{112,144}... | collective-permute-start | bytes 995336 | tf_op jit(solution)/shard_map/ppermute | solution.py:74
  60.2 16.8 %collective-permute-start.6 = (bf16[2,72,1152]{2,1,0:T(8,128)(2,1)S(1)}, bf16[2,72,1152]{2,1,0:T(8,128)(2,1)S(1)}, u32[]{:S(2)}, u32[]{:S(2)}) collective-permute-start(bf16[2,72,1152]{2,1,0:T(8,128)(2,1)S(1)} %collective-permute-done.4), channel_id=1, source_target_pairs={{0,224},{16,240},{32,0},{48,16},{64,32},{80,48},{96,64},{112,80},{... | collective-permute-start | bytes 995336 | tf_op jit(solution)/shard_map/ppermute | solution.py:74
  75.1 10.0 %collective-permute-start.7 = (bf16[2,72,640]{2,1,0:T(8,128)(2,1)S(1)}, bf16[2,72,640]{2,1,0:T(8,128)(2,1)S(1)}, u32[]{:S(2)}, u32[]{:S(2)}) collective-permute-start(bf16[2,72,640]{2,1,0:T(8,128)(2,1)S(1)} %slice.202), channel_id=1, source_target_pairs={{0,32},{16,48},{32,64},{48,80},{64,96},{80,112},{96,128},{112,144}... | collective-permute-start | bytes 552968 | tf_op jit(solution)/shard_map/ppermute | solution.py:74
  77.1 8.7 %collective-permute-start.8 = (bf16[2,72,512]{2,1,0:T(8,128)(2,1)S(1)}, bf16[2,72,512]{2,1,0:T(8,128)(2,1)S(1)}, u32[]{:S(2)}, u32[]{:S(2)}) collective-permute-start(bf16[2,72,512]{2,1,0:T(8,128)(2,1)S(1)} %slice.203), channel_id=1, source_target_pairs={{0,224},{16,240},{32,0},{48,16},{64,32},{80,48},{96,64},{112,80},{... | collective-permute-start | bytes 442376 | tf_op jit(solution)/shard_map/ppermute | solution.py:74
  86.5 15.3 %collective-permute-start.9 = (bf16[2,8,72,1152]{3,2,1,0:T(8,128)(2,1)}, bf16[2,8,72,1152]{3,2,1,0:T(8,128)(2,1)}, u32[]{:S(2)}, u32[]{:S(2)}) collective-permute-start(bf16[2,8,72,1152]{3,2,1,0:T(8,128)(2,1)} %bitcast_dynamic-update-slice_fusion.16), channel_id=1, source_target_pairs={{0,16},{16,0},{32,48},{48,32},{64,80},{80,64},{96,112},{112,96},{1... | collective-permute-start | bytes 7962632 | tf_op jit(solution)/shard_map/ppermute | solution.py:48
  91.3 2.4 copy-start.16
  94.2 11.3 %copy-start.2 = (bf16[2,2,256,576]{2,3,1,0:T(8,128)(2,1)}, bf16[2,2,256,576]{2,3,1,0:T(8,128)(2,1)S(1)}, u32[]{:S(2)}) copy-start(bf16[2,2,256,576]{2,3,1,0:T(8,128)(2,1)S(1)} %reverse_select_fusion) | copy-start | bytes 3538948
  99.3 4.5 %copy-start.6 = (bf16[1,8,72,1152]{3,2,1,0:T(8,128)(2,1)S(1)}, bf16[1,8,72,1152]{3,2,1,0:T(8,128)(2,1)}, u32[]{:S(2)}) copy-start(bf16[1,8,72,1152]{3,2,1,0:T(8,128)(2,1)} %get-tuple-element.4) | copy-start | bytes 3981316
  99.3 7.8 %collective-permute-start.11 = (bf16[8,2,72,640]{3,2,0,1:T(8,128)(2,1)S(1)}, bf16[8,2,72,640]{3,2,0,1:T(8,128)(2,1)S(1)}, u32[]{:S(2)}, u32[]{:S(2)}) collective-permute-start(bf16[8,2,72,640]{3,2,0,1:T(8,128)(2,1)S(1)} %copy.151), channel_id=1, source_target_pairs={{0,16},{16,0},{32,48},{48,32},{64,80},{80,64},{96,112},{112,96},{1... | collective-permute-start | bytes 4423688 | tf_op jit(solution)/shard_map/ppermute | solution.py:48
  106.6 1.1 copy-start.4
  106.6 1.8 copy-start.5
  110.8 14.5 %collective-permute-start.12 = (bf16[64,1152]{1,0:T(8,128)(2,1)S(1)}, bf16[64,1152]{1,0:T(8,128)(2,1)S(1)}, u32[]{:S(2)}, u32[]{:S(2)}) collective-permute-start(bf16[64,1152]{1,0:T(8,128)(2,1)S(1)} %get-tuple-element.23), channel_id=1, source_target_pairs={{0,1},{1,2},{2,3},{3,0},{4,5},{5,6},{6,7},{7,4},{8,9},{9,10},{10,1... | collective-permute-start | bytes 442376 | tf_op jit(solution)/shard_map/ppermute | solution.py:103
  113.9 13.3 %collective-permute-start.14 = (bf16[64,1152]{1,0:T(8,128)(2,1)S(1)}, bf16[64,1152]{1,0:T(8,128)(2,1)S(1)}, u32[]{:S(2)}, u32[]{:S(2)}) collective-permute-start(bf16[64,1152]{1,0:T(8,128)(2,1)S(1)} %get-tuple-element.24), channel_id=1, source_target_pairs={{0,3},{1,0},{2,1},{3,2},{4,7},{5,4},{6,5},{7,6},{8,11},{9,8},{10,9... | collective-permute-start | bytes 442376 | tf_op jit(solution)/shard_map/ppermute | solution.py:103
  118.0 14.5 %collective-permute-start.24 = (bf16[64,1152]{1,0:T(8,128)(2,1)S(1)}, bf16[64,1152]{1,0:T(8,128)(2,1)S(1)}, u32[]{:S(2)}, u32[]{:S(2)}) collective-permute-start(bf16[64,1152]{1,0:T(8,128)(2,1)S(1)} %get-tuple-element.21), channel_id=1, source_target_pairs={{0,1},{1,2},{2,3},{3,0},{4,5},{5,6},{6,7},{7,4},{8,9},{9,10},{10,1... | collective-permute-start | bytes 442376 | tf_op jit(solution)/shard_map/ppermute | solution.py:103
  119.9 14.5 %collective-permute-start.26 = (bf16[64,1152]{1,0:T(8,128)(2,1)S(1)}, bf16[64,1152]{1,0:T(8,128)(2,1)S(1)}, u32[]{:S(2)}, u32[]{:S(2)}) collective-permute-start(bf16[64,1152]{1,0:T(8,128)(2,1)S(1)} %get-tuple-element.22), channel_id=1, source_target_pairs={{0,3},{1,0},{2,1},{3,2},{4,7},{5,4},{6,5},{7,6},{8,11},{9,8},{10,9... | collective-permute-start | bytes 442376 | tf_op jit(solution)/shard_map/ppermute | solution.py:103
  125.3 14.6 %collective-permute-start.13 = (bf16[64,2304]{1,0:T(8,128)(2,1)S(1)}, bf16[64,2304]{1,0:T(8,128)(2,1)S(1)}, u32[]{:S(2)}, u32[]{:S(2)}) collective-permute-start(bf16[64,2304]{1,0:T(8,128)(2,1)S(1)} %pad_maximum_fusion.7), channel_id=1, source_target_pairs={{0,1},{1,2},{2,3},{3,0},{4,5},{5,6},{6,7},{7,4},{8,9},{9,10},{10,1... | collective-permute-start | bytes 884744 | tf_op jit(solution)/shard_map/ppermute | solution.py:103
  127.3 12.6 %collective-permute-start.15 = (bf16[64,2304]{1,0:T(8,128)(2,1)S(1)}, bf16[64,2304]{1,0:T(8,128)(2,1)S(1)}, u32[]{:S(2)}, u32[]{:S(2)}) collective-permute-start(bf16[64,2304]{1,0:T(8,128)(2,1)S(1)} %pad_maximum_fusion.8), channel_id=1, source_target_pairs={{0,3},{1,0},{2,1},{3,2},{4,7},{5,4},{6,5},{7,6},{8,11},{9,8},{10,9... | collective-permute-start | bytes 884744 | tf_op jit(solution)/shard_map/ppermute | solution.py:103
  132.5 10.3 %collective-permute-start.25 = (bf16[64,2304]{1,0:T(8,128)(2,1)S(1)}, bf16[64,2304]{1,0:T(8,128)(2,1)S(1)}, u32[]{:S(2)}, u32[]{:S(2)}) collective-permute-start(bf16[64,2304]{1,0:T(8,128)(2,1)S(1)} %pad_maximum_fusion.9), channel_id=1, source_target_pairs={{0,1},{1,2},{2,3},{3,0},{4,5},{5,6},{6,7},{7,4},{8,9},{9,10},{10,1... | collective-permute-start | bytes 884744 | tf_op jit(solution)/shard_map/ppermute | solution.py:103
  134.6 9.6 %collective-permute-start.27 = (bf16[64,2304]{1,0:T(8,128)(2,1)S(1)}, bf16[64,2304]{1,0:T(8,128)(2,1)S(1)}, u32[]{:S(2)}, u32[]{:S(2)}) collective-permute-start(bf16[64,2304]{1,0:T(8,128)(2,1)S(1)} %pad_maximum_fusion.10), channel_id=1, source_target_pairs={{0,3},{1,0},{2,1},{3,2},{4,7},{5,4},{6,5},{7,6},{8,11},{9,8},{10,9... | collective-permute-start | bytes 884744 | tf_op jit(solution)/shard_map/ppermute | solution.py:103
  140.1 21.4 %copy-start.7 = (f32[16,2304]{1,0:T(8,128)S(1)}, f32[16,2304]{1,0:T(8,128)}, u32[]{:S(2)}) copy-start(f32[16,2304]{1,0:T(8,128)} %reshape.288) | copy-start | bytes 442372
  140.1 21.4 %copy-start.8 = (f32[16,2304]{1,0:T(8,128)S(1)}, f32[16,2304]{1,0:T(8,128)}, u32[]{:S(2)}) copy-start(f32[16,2304]{1,0:T(8,128)} %reshape.290) | copy-start | bytes 442372
  140.1 8.7 %collective-permute-start.16 = (bf16[2,16,2304]{2,1,0:T(8,128)(2,1)S(1)}, bf16[2,16,2304]{2,1,0:T(8,128)(2,1)S(1)}, u32[]{:S(2)}, u32[]{:S(2)}) collective-permute-start(bf16[2,16,2304]{2,1,0:T(8,128)(2,1)S(1)} %fusion.44), channel_id=1, source_target_pairs={{0,4},{1,5},{2,6},{3,7},{4,0},{5,1},{6,2},{7,3},{8,12},{9,13},{10,... | collective-permute-start | bytes 442376 | tf_op jit(solution)/shard_map/ppermute | solution.py:52
  144.3 9.4 %collective-permute-start.28 = (bf16[2,16,2304]{2,1,0:T(8,128)(2,1)S(1)}, bf16[2,16,2304]{2,1,0:T(8,128)(2,1)S(1)}, u32[]{:S(2)}, u32[]{:S(2)}) collective-permute-start(bf16[2,16,2304]{2,1,0:T(8,128)(2,1)S(1)} %fusion.45), channel_id=1, source_target_pairs={{0,4},{1,5},{2,6},{3,7},{4,0},{5,1},{6,2},{7,3},{8,12},{9,13},{10,... | collective-permute-start | bytes 442376 | tf_op jit(solution)/shard_map/ppermute | solution.py:52
  148.8 9.4 %collective-permute-start.17 = (bf16[16,2304]{1,0:T(8,128)(2,1)S(1)}, bf16[16,2304]{1,0:T(8,128)(2,1)S(1)}, u32[]{:S(2)}, u32[]{:S(2)}) collective-permute-start(bf16[16,2304]{1,0:T(8,128)(2,1)S(1)} %fusion.61), channel_id=1, source_target_pairs={{0,8},{1,9},{2,10},{3,11},{4,12},{5,13},{6,14},{7,15},{8,0},{9,1},... | collective-permute-start | bytes 221192 | tf_op jit(solution)/shard_map/ppermute | solution.py:52
  153.8 7.6 %collective-permute-start.29 = (bf16[16,2304]{1,0:T(8,128)(2,1)S(1)}, bf16[16,2304]{1,0:T(8,128)(2,1)S(1)}, u32[]{:S(2)}, u32[]{:S(2)}) collective-permute-start(bf16[16,2304]{1,0:T(8,128)(2,1)S(1)} %fusion.62), channel_id=1, source_target_pairs={{0,8},{1,9},{2,10},{3,11},{4,12},{5,13},{6,14},{7,15},{8,0},{9,1},... | collective-permute-start | bytes 221192 | tf_op jit(solution)/shard_map/ppermute | solution.py:52
  161.6 7.3 %collective-permute-start.30 = (bf16[16,2304]{1,0:T(8,128)(2,1)S(1)}, bf16[16,2304]{1,0:T(8,128)(2,1)}, u32[]{:S(2)}, u32[]{:S(2)}) collective-permute-start(bf16[16,2304]{1,0:T(8,128)(2,1)S(1)} %get-tuple-element.27), channel_id=1, source_target_pairs={{0,8},{1,9},{2,10},{3,11},{4,12},{5,13},{6,14},{7,15},{8,0},{9,1},... | collective-permute-start | bytes 221192 | tf_op jit(solution)/shard_map/ppermute | solution.py:52
  164.3 7.8 %collective-permute-start.18 = (bf16[16,2304]{1,0:T(8,128)(2,1)S(1)}, bf16[16,2304]{1,0:T(8,128)(2,1)S(1)}, u32[]{:S(2)}, u32[]{:S(2)}) collective-permute-start(bf16[16,2304]{1,0:T(8,128)(2,1)S(1)} %get-tuple-element.28), channel_id=1, source_target_pairs={{0,8},{1,9},{2,10},{3,11},{4,12},{5,13},{6,14},{7,15},{8,0},{9,1},... | collective-permute-start | bytes 221192 | tf_op jit(solution)/shard_map/ppermute | solution.py:52
  169.8 7.0 %collective-permute-start.31 = (bf16[2,16,2304]{2,1,0:T(8,128)(2,1)S(1)}, bf16[2,16,2304]{2,1,0:T(8,128)(2,1)S(1)}, u32[]{:S(2)}, u32[]{:S(2)}) collective-permute-start(bf16[2,16,2304]{2,1,0:T(8,128)(2,1)S(1)} %maximum_select_fusion.4), channel_id=1, source_target_pairs={{0,4},{1,5},{2,6},{3,7},{4,0},{5,1},{6,2},{7,3},{8,12},{9,13},{10,... | collective-permute-start | bytes 442376 | tf_op jit(solution)/shard_map/ppermute | solution.py:52
  172.2 11.8 %collective-permute-start.19 = (bf16[2,16,2304]{2,1,0:T(8,128)(2,1)S(1)}, bf16[2,16,2304]{2,1,0:T(8,128)(2,1)S(1)}, u32[]{:S(2)}, u32[]{:S(2)}) collective-permute-start(bf16[2,16,2304]{2,1,0:T(8,128)(2,1)S(1)} %maximum_select_fusion.3), channel_id=1, source_target_pairs={{0,4},{1,5},{2,6},{3,7},{4,0},{5,1},{6,2},{7,3},{8,12},{9,13},{10,... | collective-permute-start | bytes 442376 | tf_op jit(solution)/shard_map/ppermute | solution.py:52
  176.9 14.5 %collective-permute-start.32 = (bf16[64,2304]{1,0:T(8,128)(2,1)S(1)}, bf16[64,2304]{1,0:T(8,128)(2,1)S(1)}, u32[]{:S(2)}, u32[]{:S(2)}) collective-permute-start(bf16[64,2304]{1,0:T(8,128)(2,1)S(1)} %bitcast.224), channel_id=1, source_target_pairs={{0,1},{1,2},{2,3},{3,0},{4,5},{5,6},{6,7},{7,4},{8,9},{9,10},{10,1... | collective-permute-start | bytes 884744 | tf_op jit(solution)/shard_map/ppermute | solution.py:103
  178.9 14.5 %collective-permute-start.33 = (bf16[64,2304]{1,0:T(8,128)(2,1)S(1)}, bf16[64,2304]{1,0:T(8,128)(2,1)S(1)}, u32[]{:S(2)}, u32[]{:S(2)}) collective-permute-start(bf16[64,2304]{1,0:T(8,128)(2,1)S(1)} %bitcast.225), channel_id=1, source_target_pairs={{0,3},{1,0},{2,1},{3,2},{4,7},{5,4},{6,5},{7,6},{8,11},{9,8},{10,9... | collective-permute-start | bytes 884744 | tf_op jit(solution)/shard_map/ppermute | solution.py:103
  184.1 14.4 %collective-permute-start.20 = (bf16[64,2304]{1,0:T(8,128)(2,1)S(1)}, bf16[64,2304]{1,0:T(8,128)(2,1)S(1)}, u32[]{:S(2)}, u32[]{:S(2)}) collective-permute-start(bf16[64,2304]{1,0:T(8,128)(2,1)S(1)} %bitcast.227), channel_id=1, source_target_pairs={{0,1},{1,2},{2,3},{3,0},{4,5},{5,6},{6,7},{7,4},{8,9},{9,10},{10,1... | collective-permute-start | bytes 884744 | tf_op jit(solution)/shard_map/ppermute | solution.py:103
  186.0 14.5 %collective-permute-start.21 = (bf16[64,2304]{1,0:T(8,128)(2,1)S(1)}, bf16[64,2304]{1,0:T(8,128)(2,1)S(1)}, u32[]{:S(2)}, u32[]{:S(2)}) collective-permute-start(bf16[64,2304]{1,0:T(8,128)(2,1)S(1)} %bitcast.228), channel_id=1, source_target_pairs={{0,3},{1,0},{2,1},{3,2},{4,7},{5,4},{6,5},{7,6},{8,11},{9,8},{10,9... | collective-permute-start | bytes 884744 | tf_op jit(solution)/shard_map/ppermute | solution.py:103
  191.4 17.4 %collective-permute-start.34 = (bf16[64,1152]{1,0:T(8,128)(2,1)S(1)}, bf16[64,1152]{1,0:T(8,128)(2,1)S(1)}, u32[]{:S(2)}, u32[]{:S(2)}) collective-permute-start(bf16[64,1152]{1,0:T(8,128)(2,1)S(1)} %slice.229), channel_id=1, source_target_pairs={{0,1},{1,2},{2,3},{3,0},{4,5},{5,6},{6,7},{7,4},{8,9},{9,10},{10,1... | collective-permute-start | bytes 442376 | tf_op jit(solution)/shard_map/ppermute | solution.py:103
  193.4 16.0 %collective-permute-start.35 = (bf16[64,1152]{1,0:T(8,128)(2,1)S(1)}, bf16[64,1152]{1,0:T(8,128)(2,1)S(1)}, u32[]{:S(2)}, u32[]{:S(2)}) collective-permute-start(bf16[64,1152]{1,0:T(8,128)(2,1)S(1)} %slice.230), channel_id=1, source_target_pairs={{0,3},{1,0},{2,1},{3,2},{4,7},{5,4},{6,5},{7,6},{8,11},{9,8},{10,9... | collective-permute-start | bytes 442376 | tf_op jit(solution)/shard_map/ppermute | solution.py:103
  198.6 8.2 %collective-permute-start.22 = (bf16[64,1152]{1,0:T(8,128)(2,1)S(1)}, bf16[64,1152]{1,0:T(8,128)(2,1)S(1)}, u32[]{:S(2)}, u32[]{:S(2)}) collective-permute-start(bf16[64,1152]{1,0:T(8,128)(2,1)S(1)} %slice.220), channel_id=1, source_target_pairs={{0,1},{1,2},{2,3},{3,0},{4,5},{5,6},{6,7},{7,4},{8,9},{9,10},{10,1... | collective-permute-start | bytes 442376 | tf_op jit(solution)/shard_map/ppermute | solution.py:103
  200.5 7.8 %collective-permute-start.23 = (bf16[64,1152]{1,0:T(8,128)(2,1)S(1)}, bf16[64,1152]{1,0:T(8,128)(2,1)S(1)}, u32[]{:S(2)}, u32[]{:S(2)}) collective-permute-start(bf16[64,1152]{1,0:T(8,128)(2,1)S(1)} %slice.221), channel_id=1, source_target_pairs={{0,3},{1,0},{2,1},{3,2},{4,7},{5,4},{6,5},{7,6},{8,11},{9,8},{10,9... | collective-permute-start | bytes 442376 | tf_op jit(solution)/shard_map/ppermute | solution.py:103
  213.7 1.3 copy-start.3
  216.1 5.5 %collective-permute-start.37 = (bf16[8,72,864]{2,1,0:T(8,128)(2,1)S(1)}, bf16[8,72,864]{2,1,0:T(8,128)(2,1)S(1)}, u32[]{:S(2)}, u32[]{:S(2)}) collective-permute-start(bf16[8,72,864]{2,1,0:T(8,128)(2,1)S(1)} %bitcast.230), channel_id=1, source_target_pairs={{0,16},{16,0},{32,48},{48,32},{64,80},{80,64},{96,112},{112,96},{1... | collective-permute-start | bytes 2985992 | tf_op jit(solution)/shard_map/ppermute | solution.py:48
  219.2 4.7 %collective-permute-start.36 = (bf16[8,72,864]{2,1,0:T(8,128)(2,1)S(1)}, bf16[8,72,864]{2,1,0:T(8,128)(2,1)S(1)}, u32[]{:S(2)}, u32[]{:S(2)}) collective-permute-start(bf16[8,72,864]{2,1,0:T(8,128)(2,1)S(1)} %bitcast.231), channel_id=1, source_target_pairs={{0,16},{16,0},{32,48},{48,32},{64,80},{80,64},{96,112},{112,96},{1... | collective-permute-start | bytes 2985992 | tf_op jit(solution)/shard_map/ppermute | solution.py:48
  225.5 41.1 %all-to-all-start = ((bf16[8,72,1152]{2,1,0:T(8,128)(2,1)}), bf16[8,72,1152]{2,1,0:T(8,128)(2,1)S(1)}, u32[]{:S(2)}, u32[]{:S(2)}) async-start(bf16[8,72,1152]{2,1,0:T(8,128)(2,1)} %pad_maximum_fusion.2), calls=%async_computation | async-start | bytes 2654208 | tf_op jit(solution)/shard_map/all_to_all | solution.py:69
  230.5 50.6 %reduce-scatter.4.cloned.1.call-start = ((), (), s32[]{:S(2)}) async-start(), calls=%async_computation.3 | async-start | bytes 829440
  231.8 50.4 %copy-start.9 = (bf16[288,72]{0,1:T(8,128)(2,1)S(1)}, bf16[288,72]{0,1:T(8,128)(2,1)}, u32[]{:S(2)}) copy-start(bf16[288,72]{0,1:T(8,128)(2,1)} %param.22) | copy-start | bytes 124420
  231.8 50.4 %copy-start.12 = (f32[288,72]{0,1:T(8,128)S(1)}, f32[288,72]{0,1:T(8,128)}, u32[]{:S(2)}) copy-start(f32[288,72]{0,1:T(8,128)} %param.25) | copy-start | bytes 248836
  231.8 51.2 %copy-start.10 = (bf16[72,288]{1,0:T(8,128)(2,1)S(1)}, bf16[72,288]{1,0:T(8,128)(2,1)}, u32[]{:S(2)}) copy-start(bf16[72,288]{1,0:T(8,128)(2,1)} %param.20) | copy-start | bytes 124420
  231.9 51.1 %copy-start.11 = (bf16[72,288]{1,0:T(8,128)(2,1)S(1)}, bf16[72,288]{1,0:T(8,128)(2,1)}, u32[]{:S(2)}) copy-start(bf16[72,288]{1,0:T(8,128)(2,1)} %param.21) | copy-start | bytes 124420
  231.9 51.1 %copy-start.13 = (f32[72,288]{1,0:T(8,128)S(1)}, f32[72,288]{1,0:T(8,128)}, u32[]{:S(2)}) copy-start(f32[72,288]{1,0:T(8,128)} %param.24) | copy-start | bytes 248836
  231.9 51.1 %copy-start.14 = (f32[72,288]{1,0:T(8,128)S(1)}, f32[72,288]{1,0:T(8,128)}, u32[]{:S(2)}) copy-start(f32[72,288]{1,0:T(8,128)} %param.23) | copy-start | bytes 248836
  266.6 17.1 %copy-start.1 = (bf16[256,2304]{1,0:T(8,128)(2,1)S(1)}, bf16[256,2304]{1,0:T(8,128)(2,1)}, u32[]{:S(2)}) copy-start(bf16[256,2304]{1,0:T(8,128)(2,1)} %param.14) | copy-start | bytes 3538948
  266.8 15.3 %collective-permute-start.38 = (bf16[72,864]{1,0:T(8,128)(2,1)S(1)}, bf16[72,864]{1,0:T(8,128)(2,1)S(1)}, u32[]{:S(2)}, u32[]{:S(2)}) collective-permute-start(bf16[72,864]{1,0:T(8,128)(2,1)S(1)} %slice.338), channel_id=1, source_target_pairs={{0,256},{16,272},{32,288},{48,304},{64,320},{80,336},{96,352},{112... | collective-permute-start | bytes 373256 | tf_op jit(solution)/shard_map/ppermute | solution.py:48
Sparse Core Ops, SparseCore 0:
  41.3 45.1 all-gather.2
  234.2 46.8 reduce-scatter.3
